TPU v7x, 128 devices: a whole 4x4x4 slice. The times are simulated.
128 devices in a mesh: section: 2 (over core), dp: 8 (over z, x_lo), tensor: 8 (over y, x_hi).
Axes of the slice: x: 4 (x_hi: 2, x_lo: 2; x = x_hi * 2 + x_lo), y: 4, z: 4, core: 2. Of those that a mesh axis runs over, the one named last changes fastest.
Arguments:
- upstream: bfloat16 [2, 512, 8192], P('section', ('dp', 'tensor')), may hold values from -1.5 to 1.5
- saved_input: bfloat16 [2, 512, 8192], P('section', ('dp', 'tensor')), may hold values from -400 to 400
- norm_gain: bfloat16 [2, 8192], P('section'), may hold values from 0.099609375 to 1.8984375
- up_weight: bfloat16 [2, 8192, 16384], P('section', None, ('dp', 'tensor')), may hold values from -0.0625 to 0.0625
- down_weight: bfloat16 [2, 16384, 8192], P('section', ('dp', 'tensor')), may hold values from -0.046875 to 0.046875
Outputs:
- input_grad: bfloat16 [2, 512, 8192], P('section', ('dp', 'tensor'))
- up_grad: float32 [2, 8192, 16384], P('section', None, ('dp', 'tensor'))
- down_grad: float32 [2, 16384, 8192], P('section', ('dp', 'tensor'))
- gain_grad: float32 [2, 8192], P('section')
All inputs are finite; a program needn't handle non-finite values.
Results may differ from a plain program's by a relative error of at most 0.015.
Values may be sent and summed in bfloat16 or wider, within the bound.
A program may use at most 128 MiB of HBM per device.

v0:
```python
import jax
import jax.numpy as jnp
from jax import lax
from jax.sharding import PartitionSpec as P

gelu_scale = 0.7978845608028654
cubic_coef = 0.044715


def from_partner(value, axis, apart):
    mask = 2**apart
    pairs = [(source, source ^ mask) for source in range(lax.axis_size(axis))]
    return lax.ppermute(value, axis, pairs)


def gelu_pair(hidden):
    tanh_part = jnp.tanh(gelu_scale * (hidden + cubic_coef * hidden * hidden * hidden))
    gelu_out = 0.5 * hidden * (1.0 + tanh_part)
    derivative = 0.5 * (1.0 + tanh_part) + 0.5 * hidden * (
        1.0 - tanh_part * tanh_part
    ) * gelu_scale * (1.0 + 3.0 * cubic_coef * hidden * hidden)
    return (gelu_out, derivative)


def normalize(row_values):
    row_mean = jnp.mean(row_values, axis=-1, keepdims=True)
    centered = row_values - row_mean
    variance = jnp.mean(centered * centered, axis=-1, keepdims=True)
    inverse = lax.rsqrt(variance + 1e-05)
    return (centered * inverse, inverse)


def reorder(tokens_full, grid_side):
    tok_count = tokens_full.shape[0]
    feat_width = tokens_full.shape[1]
    token_blocks = tokens_full.reshape(
        grid_side, grid_side, tok_count // (grid_side * grid_side), feat_width
    )
    return jnp.swapaxes(token_blocks, 0, 1).reshape(tok_count, feat_width)


def on_device(upstream, saved_input, norm_gain, up_weight, down_weight):
    grid_side = lax.axis_size("dp")
    rows_here = saved_input.shape[1]
    gain_wide = norm_gain[0].astype(jnp.float32)
    unit_rows, inverse = normalize(saved_input[0].astype(jnp.float32))
    normed = (unit_rows * gain_wide).astype(jnp.bfloat16)
    arriving = upstream[0]
    crossed = from_partner(arriving, "section", 0)
    normed_full, grad_full = (
        lax.all_gather(normed, ("dp", "tensor"), axis=0, tiled=True),
        lax.all_gather(crossed, ("dp", "tensor"), axis=0, tiled=True),
    )
    grad_mine = reorder(grad_full, grid_side)
    up_block = up_weight[0]
    hidden = jnp.dot(normed_full, up_block, preferred_element_type=jnp.float32)
    act_value, derivative = gelu_pair(hidden)
    activation = act_value.astype(jnp.bfloat16)
    grad_act = lax.dot_general(
        grad_mine, down_weight[0], (((1,), (1,)), ((), ())), preferred_element_type=jnp.float32
    )
    grad_hidden = (grad_act * derivative).astype(jnp.bfloat16)
    down_grad = lax.dot_general(
        activation, grad_mine, (((0,), (0,)), ((), ())), preferred_element_type=jnp.float32
    )
    up_grad = lax.dot_general(
        normed_full, grad_hidden, (((0,), (0,)), ((), ())), preferred_element_type=jnp.float32
    )
    grad_normed = lax.psum_scatter(
        lax.dot_general(
            grad_hidden, up_block, (((1,), (1,)), ((), ())), preferred_element_type=jnp.float32
        ),
        ("dp", "tensor"),
        scatter_dimension=0,
        tiled=True,
    )
    gain_part = jnp.sum(grad_normed * unit_rows, axis=0)
    grad_scaled = grad_normed * gain_wide
    inner_mean = jnp.mean(grad_scaled, axis=-1, keepdims=True)
    proj_mean = jnp.mean(grad_scaled * unit_rows, axis=-1, keepdims=True)
    grad_input = inverse * (grad_scaled - inner_mean - unit_rows * proj_mean)
    own_grad = lax.dynamic_slice_in_dim(
        grad_mine, lax.axis_index(("dp", "tensor")) * rows_here, rows_here, 0
    )
    result = (own_grad.astype(jnp.float32) + grad_input).astype(jnp.bfloat16)
    gain_total = lax.psum(gain_part, ("dp", "tensor"))
    return (result[None], up_grad[None], down_grad[None], gain_total[None])


def solution(mesh):
    in_specs = (
        P("section", ("dp", "tensor"), None),
        P("section", ("dp", "tensor"), None),
        P("section", None),
        P("section", None, ("dp", "tensor")),
        P("section", ("dp", "tensor"), None),
    )
    out_specs = (
        P("section", ("dp", "tensor"), None),
        P("section", None, ("dp", "tensor")),
        P("section", ("dp", "tensor"), None),
        P("section", None),
    )
    return jax.shard_map(
        on_device, mesh=mesh, in_specs=in_specs, out_specs=out_specs, check_vma=False
    )
```

profile of v0, /device:TPU:0, one launch (start us, length us, event | category | flops | bytes accessed | tf_op | source)
XLA Modules:
  0.0 1552.9 jit_solution(12888842941920125523)
XLA Ops:
  7.2 0.0 all-gather.5.cloned.1.call-start
  7.2 1.1 convert_reduce_fusion
  8.3 1.2 fusion.31
  9.5 0.8 mul.136
  10.3 1.7 fusion.24
  11.9 0.0 all-gather.5.cloned.1.call-update
  12.0 0.0 all-gather.3.cloned.1.call-start
  12.0 0.1 collective-permute-start
  12.1 1.5 collective-permute-done
  13.6 0.0 copy-start.2
  13.6 0.7 copy-done.2
  14.3 0.0 all-gather.3.cloned.1.call-update
  14.3 0.0 reduce-scatter.2.cloned.1.call-start
  14.4 355.0 %all-gather.5.cloned.1.call-done = bf16[512,8192]{1,0:T(8,128)(2,1)} async-done(((bf16[8,8192]{1,0:T(8,128)(2,1)}), bf16[512,8192]{1,0:T(8,128)(2,1)}) %all-gather.5.cloned.1.call-update) | async-done | bytes 8388624 | tf_op jit(solution)/shard_map/all_gather | solution.py:51
  369.3 6.9 fusion.2
  376.3 350.3 %all-gather.3.cloned.1.call-done = bf16[512,8192]{1,0:T(8,128)(2,1)} async-done(((bf16[8,8192]{1,0:T(8,128)(2,1)}), bf16[512,8192]{1,0:T(8,128)(2,1)}) %all-gather.3.cloned.1.call-update) | async-done | bytes 8388624 | tf_op jit(solution)/shard_map/all_gather | solution.py:52
  726.6 7.6 copy.9
  734.2 0.0 copy-start
  734.2 7.2 fusion.9
  741.4 0.0 copy-done
  741.4 8.1 fusion
  749.5 0.0 reduce-scatter.2.cloned.1.call-update
  749.6 9.2 convolution_bitcast_fusion
  758.8 0.0 copy-start.1
  758.8 9.2 convolution_bitcast_fusion.1
  768.0 431.2 %reduce-scatter.2.cloned.1.call-done = f32[8,8192]{1,0:T(8,128)} async-done(((f32[512,8192]{1,0:T(8,128)}), f32[8,8192]{1,0:T(8,128)}) %reduce-scatter.2.cloned.1.call-update) | async-done | bytes 262160 | tf_op jit(solution)/shard_map/reduce_scatter | solution.py:69
  1199.2 0.0 copy-done.1
  1199.2 1.3 fusion.30
  1200.5 344.2 %psum.7 = f32[1,8192]{1,0:T(1,128)} all-reduce(f32[1,8192]{1,0:T(1,128)S(1)} %bitcast.72), channel_id=1, replica_groups=mesh['section'=2,'dp'=8,'tensor'=8] {'dp','tensor'}, use_global_device_ids=true, to_apply=%region_6.0 | all-reduce | flops 8192 | bytes 65536 | tf_op jit(solution)/shard_map/psum | solution.py:86
  1544.6 1.8 fusion.36
  (3 shorter events, 0.0 us)
Async XLA Ops:
  7.2 362.2 %all-gather.5.cloned.1.call-start = ((), (), s32[]{:S(2)}) async-start(), calls=%async_computation.2 | async-start | bytes 8519680 | tf_op jit(solution)/shard_map/all_gather | solution.py:51
  12.0 714.6 %all-gather.3.cloned.1.call-start = ((), (), s32[]{:S(2)}) async-start(), calls=%async_computation.1 | async-start | bytes 8519680 | tf_op jit(solution)/shard_map/all_gather | solution.py:52
  12.0 1.6 collective-permute-start
  13.6 0.7 copy-start.2
  14.3 1184.8 %reduce-scatter.2.cloned.1.call-start = ((), (), s32[]{:S(2)}) async-start(), calls=%async_computation.3 | async-start | bytes 17039360 | tf_op jit(solution)/shard_map/reduce_scatter | solution.py:69
  734.2 7.2 copy-start
  758.8 440.4 %copy-start.1 = (bf16[1,8,8192]{2,1,0:T(8,128)(2,1)S(1)}, bf16[1,8,8192]{2,1,0:T(8,128)(2,1)}, u32[]{:S(2)}) copy-start(bf16[1,8,8192]{2,1,0:T(8,128)(2,1)} %param.6) | copy-start | bytes 393220
Sparse Core Ops, SparseCore 0:
  12.1 357.2 all-gather.4
  371.6 354.9 all-gather.2
  749.7 449.4 reduce-scatter.1
where the time goes:
time: 1550 us
  waiting for transfers between devices  1140 us (74%)
  blocking collectives  344 us (22%)
  matrix products  40.7 us (3%)
    reduce_scatter x1, waiting for transfers between devices, on_device(): lax.psum_scatter(lax.dot_general(grad_hidden, up_block, (((1,), (1,)), ((...  431 us
    all_gather x1, waiting for transfers between devices, on_device(): lax.all_gather(normed, ('dp', 'tensor'), axis=0, tiled=True)  355 us
    all_gather x1, waiting for transfers between devices, on_device(): lax.all_gather(crossed, ('dp', 'tensor'), axis=0, tiled=True)  350 us
    psum x1, blocking collectives, on_device(): gain_total = lax.psum(gain_part, ('dp', 'tensor'))  344 us
  transfers between devices with their start and end apart: 4, of which 4 were waited for; matrix products, arithmetic and copies ran while one was open for 2% of the time, Pallas kernels for 0%

commit v1 on v0

v1 whole, which is shorter than its diff:
```python
import jax
import jax.numpy as jnp
from jax import lax
from jax.experimental import pallas as pl
from jax.experimental.pallas import tpu as pltpu
from jax.sharding import PartitionSpec as P

gelu_scale = 0.7978845608028654
cubic_coef = 0.044715

D = 8192
HALF = D // 2
HID = 256
ROWS = 8
MESH = pl.DeviceIdType.MESH

ORDERS = ((2, 1, 0), (0, 2, 1), (1, 0, 2))


def cut(tiles):
    subs, at = [], 0
    for number, count in enumerate(tiles):
        subs.append((ORDERS[number // 2], 1 if number % 2 == 0 else -1, at * 128, count * 128))
        at += count
    return tuple(subs)


GATHER = cut((11, 11, 11, 10, 11, 10))
SCATTER = cut((6, 5, 6, 5, 5, 5))
SUBS = range(6)


def gelu_pair(hidden):
    tanh_part = jnp.tanh(gelu_scale * (hidden + cubic_coef * hidden * hidden * hidden))
    gelu_out = 0.5 * hidden * (1.0 + tanh_part)
    derivative = 0.5 * (1.0 + tanh_part) + 0.5 * hidden * (
        1.0 - tanh_part * tanh_part
    ) * gelu_scale * (1.0 + 3.0 * cubic_coef * hidden * hidden)
    return (gelu_out, derivative)


def f32(value):
    return value.astype(jnp.float32)


def kernel(
    upstream, saved, gain, up_hbm, down_hbm,
    input_grad, gain_grad, up_grad, down_grad,
    tokens, up, down, part, got0, got1, got2, hid, weights, sent_rows, arrived_rows, unit, total, gain_acc, gain_slots,
    up_stage, down_stage,
    load_sem, swap_sem, stage_sem, ag_send, ag_recv, rs_send, rs_recv, gain_send, gain_recv,
):
    section = lax.axis_index("section")
    dp = lax.axis_index("dp")
    tensor = lax.axis_index("tensor")
    place = (dp // 2, tensor // 2, (tensor % 2) * 2 + dp % 2)

    def device_at(z, y, x):
        return (section, z * 2 + x % 2, y * 2 + x // 2)

    def moved(axis, by):
        return lax.rem(place[axis] + (by + 4), 4)

    def neighbour(axis, by):
        there = list(place)
        there[axis] = moved(axis, by)
        return device_at(*there)

    partner = (1 - section, dp, tensor)

    barrier = pltpu.get_barrier_semaphore()
    others = [neighbour(axis, by) for axis in range(3) for by in (1, 2, 3)] + [partner]
    for other in others:
        pl.semaphore_signal(barrier, inc=1, device_id=other, device_id_type=MESH)
    load_up = pltpu.make_async_copy(up_hbm, up, load_sem.at[0])
    load_down = pltpu.make_async_copy(down_hbm, down, load_sem.at[1])
    load_up.start()
    load_down.start()
    sent_rows[...] = f32(upstream[...])
    pl.semaphore_wait(barrier, len(others))

    swap = pltpu.make_async_remote_copy(
        src_ref=sent_rows, dst_ref=arrived_rows, send_sem=swap_sem.at[0], recv_sem=swap_sem.at[1],
        device_id=partner, device_id_type=MESH,
    )
    swap.start()

    rows = f32(saved[...])
    centered = rows - jnp.mean(rows, axis=-1, keepdims=True)
    inverse = lax.rsqrt(jnp.mean(centered * centered, axis=-1, keepdims=True) + 1e-05)
    unit[...] = centered * inverse
    normed = unit[...] * f32(gain[...])
    swap.wait_recv()
    tokens[place[0], place[1], place[2]] = jnp.concatenate([normed, arrived_rows[...]], axis=0).astype(jnp.bfloat16)

    hid[...] = jnp.zeros_like(hid)

    def gathered(phase, sub, where):
        order, _, lo, size = GATHER[sub]
        index = [slice(None)] * 3
        for later in range(phase, 3):
            index[order[later]] = place[order[later]]
        index[order[phase]] = where
        return tokens.at[(*index, slice(None), pl.ds(lo, size))]

    def ag_copy(phase, sub, message, where, by):
        block = gathered(phase, sub, where)
        return pltpu.make_async_remote_copy(
            src_ref=block, dst_ref=block,
            send_sem=ag_send.at[phase, sub, message], recv_sem=ag_recv.at[phase, sub, message],
            device_id=neighbour(GATHER[sub][0][phase], by), device_id_type=MESH,
        )

    def ag_start(phase, sub):
        axis, way = GATHER[sub][0][phase], GATHER[sub][1]
        ag_copy(phase, sub, 0, place[axis], way).start()
        ag_copy(phase, sub, 1, place[axis], -way).start()

    def ag_forward(phase, sub):
        axis, way = GATHER[sub][0][phase], GATHER[sub][1]
        copy = ag_copy(phase, sub, 0, moved(axis, -way), way)
        copy.wait_recv()
        ag_copy(phase, sub, 2, moved(axis, -way), way).start()

    def ag_wait(phase, sub, message):
        axis, way = GATHER[sub][0][phase], GATHER[sub][1]
        ag_copy(phase, sub, message, moved(axis, way if message == 1 else 2), way).wait_recv()

    def plane(order, where):
        index = [slice(None)] * 3
        index[order[2]] = where
        return tuple(index)

    def first_products(sub, where):
        order, _, lo, size = GATHER[sub]
        at = plane(order, where)
        block = tokens[(*at, slice(None), pl.ds(lo, size))].reshape(256, size)
        above = jnp.dot(block, up[pl.ds(lo, size), :], preferred_element_type=jnp.float32)
        hid[(*at, pl.ds(0, 8), pl.ds(0, HID))] += above.reshape(4, 4, 16, HID)[:, :, :8]
        below = lax.dot_general(
            block, down[:, pl.ds(lo, size)], (((1,), (1,)), ((), ())), preferred_element_type=jnp.float32
        )
        hid[(*at, pl.ds(8, 8), pl.ds(HID, HID))] += below.reshape(4, 4, 16, HID)[:, :, 8:]

    for sub in SUBS:
        ag_start(0, sub)
    for phase in (0, 1):
        for sub in SUBS:
            ag_forward(phase, sub)
        for sub in SUBS:
            ag_wait(phase, sub, 1)
            ag_wait(phase, sub, 2)
            ag_start(phase + 1, sub)
    load_up.wait()
    load_down.wait()
    for sub in SUBS:
        first_products(sub, moved(GATHER[sub][0][2], 0))
    for sub in SUBS:
        ag_forward(2, sub)
    for sub in SUBS:
        first_products(sub, moved(GATHER[sub][0][2], -GATHER[sub][1]))
    for sub in SUBS:
        ag_wait(2, sub, 1)
        first_products(sub, moved(GATHER[sub][0][2], GATHER[sub][1]))
    for sub in SUBS:
        ag_wait(2, sub, 2)
        first_products(sub, moved(GATHER[sub][0][2], 2))

    SWAPPED = (0, 2, 1, 3)

    def activate(step, carry):
        z, y = step // 4, step % 4
        act, derivative = gelu_pair(hid[z, y, :, 0:8, 0:HID])
        for x in range(4):
            hid[z, y, x, 0:8, HID:] = hid[y, z, SWAPPED[x], 8:16, HID:] * derivative[x]
            hid[z, y, x, 0:8, 0:HID] = act[x]
        return carry

    lax.fori_loop(0, 16, activate, 0)

    def lay_out(step, carry):
        z, y = step // 4, step % 4
        blank = jnp.zeros((8, HID), jnp.float32)
        for x in range(4):
            weights[z, y, x, :, 0:HID] = jnp.concatenate([hid[z, y, x, 0:8, HID:], blank], axis=0).astype(jnp.bfloat16)
            weights[z, y, x, :, HID:] = jnp.concatenate(
                [blank, hid[y, z, SWAPPED[x], 0:8, 0:HID]], axis=0
            ).astype(jnp.bfloat16)
        return carry

    def second_products(sub, where):
        order, _, lo, size = SCATTER[sub]
        at = plane(order, where)
        left = hid[(*at, pl.ds(0, 8), pl.ds(HID, HID))].reshape(128, HID).astype(jnp.bfloat16)
        halves = []
        for start in (lo, HALF + lo):
            halves.append(
                lax.dot_general(
                    left, up[pl.ds(start, size), :], (((1,), (1,)), ((), ())), preferred_element_type=jnp.float32
                ).reshape(4, 4, 8, size)
            )
        part[(*at, slice(None), pl.ds(lo, size))] = jnp.concatenate(halves, axis=2).astype(jnp.bfloat16)

    GOT = (got0, got1, got2)

    def landing(phase, sub, message):
        _, _, lo, size = SCATTER[sub]
        ref = GOT[phase]
        return ref.at[(message, *([slice(None)] * (2 - phase)), slice(None), pl.ds(lo, size))]

    def share(phase, sub, where):
        order, _, lo, size = SCATTER[sub]
        columns = (slice(None), pl.ds(lo, size))
        if phase == 0:
            return part.at[(*plane(order, where), *columns)]
        if phase == 1:
            index = tuple(where if axis == order[1] else slice(None) for axis in range(3) if axis != order[2])
            return got0.at[(2, *index, *columns)]
        return got1.at[(2, where, *columns)]

    def rs_copy(phase, sub, message):
        order, way = SCATTER[sub][0], SCATTER[sub][1]
        axis = order[2 - phase]
        if message == 0:
            source, by = share(phase, sub, moved(axis, 2)), -way
        elif message == 1:
            source, by = share(phase, sub, moved(axis, way)), way
        else:
            source, by = landing(phase, sub, 0), -way
        return pltpu.make_async_remote_copy(
            src_ref=source, dst_ref=landing(phase, sub, message),
            send_sem=rs_send.at[phase, sub, message], recv_sem=rs_recv.at[phase, sub, message],
            device_id=neighbour(axis, by), device_id_type=MESH,
        )

    def rs_forward(phase, sub):
        order, way = SCATTER[sub][0], SCATTER[sub][1]
        rs_copy(phase, sub, 0).wait_recv()
        ref = landing(phase, sub, 0)
        mine = share(phase, sub, moved(order[2 - phase], -way))
        ref[...] = (f32(ref[...]) + f32(mine[...])).astype(jnp.bfloat16)
        rs_copy(phase, sub, 2).start()

    def rs_sum(phase, sub):
        order = SCATTER[sub][0]
        rs_copy(phase, sub, 1).wait_recv()
        rs_copy(phase, sub, 2).wait_recv()
        mine = share(phase, sub, moved(order[2 - phase], 0))
        return f32(mine[...]) + f32(landing(phase, sub, 1)[...]) + f32(landing(phase, sub, 2)[...])

    for sub in SUBS:
        second_products(sub, moved(SCATTER[sub][0][2], 2))
        rs_copy(0, sub, 0).start()
    for sub in SUBS:
        second_products(sub, moved(SCATTER[sub][0][2], SCATTER[sub][1]))
        rs_copy(0, sub, 1).start()
    for sub in SUBS:
        second_products(sub, moved(SCATTER[sub][0][2], -SCATTER[sub][1]))
    lax.fori_loop(0, 16, lay_out, 0)

    TILE = 512

    def stage_copies(step):
        slot = lax.rem(step, 2)
        at = pl.ds(pl.multiple_of(step * TILE, TILE), TILE)
        return (
            pltpu.make_async_copy(up_stage.at[slot], up_grad.at[at, :], stage_sem.at[0, slot]),
            pltpu.make_async_copy(down_stage.at[slot], down_grad.at[:, at], stage_sem.at[1, slot]),
        )

    def weight_tile(step, carry):
        slot = lax.rem(step, 2)

        @pl.when(step >= 2)
        def _():
            for copy in stage_copies(step - 2):
                copy.wait()

        block = tokens[:, :, :, :, pl.ds(pl.multiple_of(step * TILE, TILE), TILE)].reshape(1024, TILE)
        up_stage[slot] = lax.dot_general(
            block, weights[:, :, :, :, 0:HID].reshape(1024, HID), (((0,), (0,)), ((), ())),
            preferred_element_type=jnp.float32,
        )
        down_stage[slot] = lax.dot_general(
            weights[:, :, :, :, HID:].reshape(1024, HID), block, (((0,), (0,)), ((), ())),
            preferred_element_type=jnp.float32,
        )
        for copy in stage_copies(step):
            copy.start()
        return carry

    lax.fori_loop(0, 4, weight_tile, 0)
    for sub in SUBS:
        rs_forward(0, sub)
    for sub in SUBS:
        second_products(sub, moved(SCATTER[sub][0][2], 0))

    def gain_tile(step, carry):
        at = pl.ds(pl.multiple_of(step * 256, 256), 256)
        also = pl.ds(pl.multiple_of(HALF + step * 256, 256), 256)
        sums = [jnp.zeros((8, 256), jnp.float32)] * 2
        for z in range(4):
            here = f32(part[z, :, :, :, at]).reshape(16, 16, 256)
            for half, columns in enumerate((at, also)):
                rows = f32(tokens[z, :, :, :, columns]).reshape(16, 16, 256)[:, :8]
                sums[half] = sums[half] + jnp.sum(here[:, 8 * half : 8 * half + 8] * rows, axis=0)
        gain_acc[:, at] = sums[0]
        gain_acc[:, also] = sums[1]
        return carry

    lax.fori_loop(0, HALF // 256, gain_tile, 0)
    gain_slots[0, place[2]] = jnp.sum(gain_acc[...], axis=0, keepdims=True) / f32(gain[...])

    def gain_copy(phase, by, owner):
        axis = 2 - phase
        return pltpu.make_async_remote_copy(
            src_ref=gain_slots.at[phase, owner], dst_ref=gain_slots.at[phase, owner],
            send_sem=gain_send.at[phase, by - 1], recv_sem=gain_recv.at[phase, by - 1],
            device_id=neighbour(axis, by), device_id_type=MESH,
        )

    def gain_start(phase):
        for by in (1, 2, 3):
            gain_copy(phase, by, place[2 - phase]).start()

    def gain_sum(phase):
        for by in (1, 2, 3):
            gain_copy(phase, by, moved(2 - phase, -by)).wait_recv()
        return (gain_slots[phase, 0] + gain_slots[phase, 1]) + (gain_slots[phase, 2] + gain_slots[phase, 3])

    gain_start(0)
    lax.fori_loop(4, 8, weight_tile, 0)
    gain_slots[1, place[1]] = gain_sum(0)
    gain_start(1)
    lax.fori_loop(8, 12, weight_tile, 0)
    gain_slots[2, place[0]] = gain_sum(1)
    gain_start(2)
    lax.fori_loop(12, 16, weight_tile, 0)
    gain_grad[...] = gain_sum(2)

    for phase in (0, 1):
        for sub in SUBS:
            landing(phase, sub, 2)[...] = rs_sum(phase, sub).astype(jnp.bfloat16)
            rs_copy(phase + 1, sub, 0).start()
            rs_copy(phase + 1, sub, 1).start()
        for sub in SUBS:
            rs_forward(phase + 1, sub)
    for sub in SUBS:
        _, _, lo, size = SCATTER[sub]
        summed = rs_sum(2, sub)
        total[:, pl.ds(lo, size)] = summed[:8]
        total[:, pl.ds(HALF + lo, size)] = summed[8:]

    scaled = total[...] * f32(gain[...])
    units = unit[...]
    inner_mean = jnp.mean(scaled, axis=-1, keepdims=True)
    proj_mean = jnp.mean(scaled * units, axis=-1, keepdims=True)
    change = inverse * (scaled - inner_mean - units * proj_mean)
    own = f32(tokens[place[1], place[0], (place[2] % 2) * 2 + place[2] // 2])[8:]
    input_grad[...] = (own + change).astype(jnp.bfloat16)

    for step in (14, 15):
        for copy in stage_copies(step):
            copy.wait()
    swap.wait_send()
    for phase in range(3):
        for sub in SUBS:
            axis, way = GATHER[sub][0][phase], GATHER[sub][1]
            ag_copy(phase, sub, 0, place[axis], way).wait_send()
            ag_copy(phase, sub, 1, place[axis], -way).wait_send()
            ag_copy(phase, sub, 2, moved(axis, -way), way).wait_send()
            for message in range(3):
                rs_copy(phase, sub, message).wait_send()
        for by in (1, 2, 3):
            gain_copy(phase, by, place[2 - phase]).wait_send()


def on_device(upstream, saved_input, norm_gain, up_weight, down_weight):
    bf16, f4 = jnp.bfloat16, jnp.float32
    vmem, hbm = pl.BlockSpec(memory_space=pltpu.VMEM), pl.BlockSpec(memory_space=pl.ANY)
    dma = pltpu.SemaphoreType.DMA
    input_grad, gain_grad, up_grad, down_grad = pl.pallas_call(
        kernel,
        out_shape=[
            jax.ShapeDtypeStruct((ROWS, D), bf16),
            jax.ShapeDtypeStruct((1, D), f4),
            jax.ShapeDtypeStruct((D, HID), f4),
            jax.ShapeDtypeStruct((HID, D), f4),
        ],
        in_specs=[vmem, vmem, vmem, hbm, hbm],
        out_specs=[vmem, vmem, hbm, hbm],
        scratch_shapes=[
            pltpu.VMEM((4, 4, 4, 16, D), bf16),
            pltpu.VMEM((D, HID), bf16),
            pltpu.VMEM((HID, D), bf16),
            pltpu.VMEM((4, 4, 4, 16, HALF), bf16),
            pltpu.VMEM((3, 4, 4, 16, HALF), bf16),
            pltpu.VMEM((3, 4, 16, HALF), bf16),
            pltpu.VMEM((3, 16, HALF), bf16),
            pltpu.VMEM((4, 4, 4, 16, 2 * HID), f4),
            pltpu.VMEM((4, 4, 4, 16, 2 * HID), bf16),
            pltpu.VMEM((ROWS, D), f4),
            pltpu.VMEM((ROWS, D), f4),
            pltpu.VMEM((ROWS, D), f4),
            pltpu.VMEM((ROWS, D), f4),
            pltpu.VMEM((ROWS, D), f4),
            pltpu.VMEM((3, 4, 1, D), f4),
            pltpu.VMEM((2, 512, HID), f4),
            pltpu.VMEM((2, HID, 512), f4),
            dma((2,)), dma((2,)), dma((2, 2)),
            dma((3, 6, 3)), dma((3, 6, 3)), dma((3, 6, 3)), dma((3, 6, 3)),
            dma((3, 3)), dma((3, 3)),
        ],
        compiler_params=pltpu.CompilerParams(
            collective_id=0, has_side_effects=True, vmem_limit_bytes=60 * 2**20
        ),
        name="section_backward",
    )(upstream[0], saved_input[0], norm_gain, up_weight[0], down_weight[0])
    return (input_grad[None], up_grad[None], down_grad[None], gain_grad)


def solution(mesh):
    in_specs = (
        P("section", ("dp", "tensor"), None),
        P("section", ("dp", "tensor"), None),
        P("section", None),
        P("section", None, ("dp", "tensor")),
        P("section", ("dp", "tensor"), None),
    )
    out_specs = (
        P("section", ("dp", "tensor"), None),
        P("section", None, ("dp", "tensor")),
        P("section", ("dp", "tensor"), None),
        P("section", None),
    )
    return jax.shard_map(
        on_device, mesh=mesh, in_specs=in_specs, out_specs=out_specs, check_vma=False
    )
```

time: 1550 us -> 151 us (0.10)
  waiting for transfers between devices: 1140 us -> 0 us
  blocking collectives: 344 us -> 0 us
  Pallas kernels: 0 us -> 137 us
  matrix products: 40.7 us -> 0 us
    all_gather x2 -> x0, waiting for transfers between devices: 705 us -> none  [the longest x1 355 us: on_device(): lax.all_gather(normed, ('dp', 'tensor'), axis=0, tiled=True)]
    reduce_scatter x1 -> x0, waiting for transfers between devices: 431 us -> none  [on_device(): lax.psum_scatter(lax.dot_general(grad_hidden, up_block, (((1,), (1,)), ((...]
    psum x1 -> x0, blocking collectives: 344 us -> none  [on_device(): gain_total = lax.psum(gain_part, ('dp', 'tensor'))]
    pallas_call x0 -> x1, Pallas kernels: none -> 137 us  [on_device(): pl.pallas_call(kernel, out_shape=[jax.ShapeDtypeStruct((ROWS, D), bf16),...]
    dot_general x5 -> x0, matrix products: 40.7 us -> none  [the longest x1 9.23 us: on_device(): lax.dot_general(activation, grad_mine, (((0,), (0,)), ((), ())), preferre...]
  transfers between devices with their start and end apart: 4 -> 0, of which waited for: 4 -> 0; matrix products, arithmetic and copies ran while one was open for 2% -> 0% of each run, Pallas kernels for 0% -> 0%
where the time goes in v1:
time: 151 us
  Pallas kernels  137 us (91%)
  local copies, waits for them, and re-layouts  13.2 us (9%)
    pallas_call x1, Pallas kernels, on_device(): pl.pallas_call(kernel, out_shape=[jax.ShapeDtypeStruct((ROWS, D), bf16),...  137 us
    unnamed x10, local copies, waits for them, and re-layouts  13.2 us

profile of v1, /device:TPU:0, one launch (start us, length us, event | category | flops | bytes accessed | tf_op | source)
XLA Modules:
  0.0 150.9 jit_solution(296064356217462560)
XLA Ops:
  0.6 137.0 %section_backward.1 = (bf16[8,8192]{1,0:T(8,128)(2,1)}, f32[1,8192]{1,0:T(1,128)}, f32[8192,256]{1,0:T(8,128)}, f32[256,8192]{1,0:T(8,128)}) custom-call(bf16[8,8192]{1,0:T(8,128)(2,1)} %bitcast.13, bf16[8,8192]{1,0:T(8,128)(2,1)} %bitcast.14, bf16[1,8192]{1,0:T(2,128)(2,1)} %gain.1, bf16[8192,256]{1,0:T(8,128)(2,1)} %bitcast.11, bf16[256,8192]{1,0:T(8,128)(2,1)} %bitcast.12), custom_call_target="tpu_custom_call" | custom-call | tf_op jit(solution)/shard_map/section_backward/pallas_call | solution.py:382
  137.6 0.0 slice-start
  137.6 1.7 %copy.13 = bf16[1,8,8192]{2,1,0:T(8,128)(2,1)} copy(bf16[1,8,8192]{2,1,0:T(8,128)(2,1)} %bitcast.15) | data formatting | bytes 262144
  139.4 0.0 slice-start.1
  139.4 7.5 %copy.14 = f32[1,8192,256]{2,1,0:T(8,128)} copy(f32[1,8192,256]{2,1,0:T(8,128)} %bitcast.10) | data formatting | bytes 16777216
  146.9 0.0 slice-done
  146.9 0.0 slice-done.1
  146.9 0.0 copy-start
  146.9 3.4 %copy.15 = f32[1,256,8192]{2,1,0:T(8,128)} copy(f32[1,256,8192]{2,1,0:T(8,128)S(1)} %bitcast.9) | data formatting | bytes 16777216
  150.3 0.0 copy-done
  150.3 0.6 copy.16
  (1 shorter events, 0.0 us)
Async XLA Ops:
  137.6 9.2 %slice-start = ((s8[8388608]{0:T(1024)(128)(4,1)}), s8[4194304]{0:T(1024)(128)(4,1)S(1)}, s32[]{:S(2)}) async-start(s8[8388608]{0:T(1024)(128)(4,1)} %bitcast.7), calls=%async_computation | async-start | bytes 8388608
  139.4 7.5 %slice-start.1 = ((s8[8388608]{0:T(1024)(128)(4,1)}), s8[4194304]{0:T(1024)(128)(4,1)S(1)}, s32[]{:S(2)}) async-start(s8[8388608]{0:T(1024)(128)(4,1)} %bitcast.7), calls=%async_computation.1 | async-start | bytes 8388608
  146.9 3.4 %copy-start = (f32[1,8192]{1,0:T(1,128)S(1)}, f32[1,8192]{1,0:T(1,128)}, u32[]{:S(2)}) copy-start(f32[1,8192]{1,0:T(1,128)} %get-tuple-element.19) | copy-start | bytes 98308

commit v2 on v1

v2 whole, which is shorter than its diff:
```python
import jax
import jax.numpy as jnp
from jax import lax
from jax.experimental import pallas as pl
from jax.experimental.pallas import tpu as pltpu
from jax.sharding import PartitionSpec as P

gelu_scale = 0.7978845608028654
cubic_coef = 0.044715

D = 8192
HALF = D // 2
HID = 256
ROWS = 8
MESH = pl.DeviceIdType.MESH

ORDERS = ((2, 1, 0), (0, 2, 1), (1, 0, 2))


def cut(tiles):
    subs, at = [], 0
    for number, count in enumerate(tiles):
        subs.append((ORDERS[number // 2], 1 if number % 2 == 0 else -1, at * 128, count * 128))
        at += count
    return tuple(subs)


GATHER = cut((11, 11, 10, 11, 11, 10))
SCATTER = cut((6, 5, 6, 5, 5, 5))
SUBS = range(6)


def gelu_pair(hidden):
    tanh_part = jnp.tanh(gelu_scale * (hidden + cubic_coef * hidden * hidden * hidden))
    gelu_out = 0.5 * hidden * (1.0 + tanh_part)
    derivative = 0.5 * (1.0 + tanh_part) + 0.5 * hidden * (
        1.0 - tanh_part * tanh_part
    ) * gelu_scale * (1.0 + 3.0 * cubic_coef * hidden * hidden)
    return (gelu_out, derivative)


def f32(value):
    return value.astype(jnp.float32)


def kernel(
    upstream, saved, gain, up_hbm, down_hbm,
    up_grad, down_grad, total, unit, inverse, own, gain_grad,
    tokens, weights, up, part, got0, got1, got2, hid, sent_rows, arrived_rows, gain_acc, gain_slots,
    load_sem, swap_sem, ag_send, ag_recv, rs_send, rs_recv, gain_send, gain_recv,
):
    section = lax.axis_index("section")
    dp = lax.axis_index("dp")
    tensor = lax.axis_index("tensor")
    place = (dp // 2, tensor // 2, (tensor % 2) * 2 + dp % 2)
    started = []

    def go(copy):
        copy.start()
        started.append(copy)

    def device_at(z, y, x):
        return (section, z * 2 + x % 2, y * 2 + x // 2)

    def moved(axis, by):
        return lax.rem(place[axis] + (by + 4), 4)

    def neighbour(axis, by):
        there = list(place)
        there[axis] = moved(axis, by)
        return device_at(*there)

    partner = (1 - section, dp, tensor)

    barrier = pltpu.get_barrier_semaphore()
    others = [neighbour(axis, by) for axis in range(3) for by in (1, 2, 3)] + [partner]
    for other in others:
        pl.semaphore_signal(barrier, inc=1, device_id=other, device_id_type=MESH)
    sent_rows[...] = f32(upstream[...])
    rows = f32(saved[...])
    centered = rows - jnp.mean(rows, axis=-1, keepdims=True)
    spread = lax.rsqrt(jnp.mean(centered * centered, axis=-1, keepdims=True) + 1e-05)
    inverse[...] = jnp.broadcast_to(spread, inverse.shape)
    unit[...] = centered * spread
    pl.semaphore_wait(barrier, len(others))

    swap = pltpu.make_async_remote_copy(
        src_ref=sent_rows, dst_ref=arrived_rows, send_sem=swap_sem.at[0], recv_sem=swap_sem.at[1],
        device_id=partner, device_id_type=MESH,
    )
    go(swap)
    normed = unit[...] * f32(gain[...])
    swap.wait_recv()
    tokens[place[0], place[1], place[2]] = jnp.concatenate([normed, arrived_rows[...]], axis=0).astype(jnp.bfloat16)

    def gathered(phase, sub, unit_by, where):
        order, _, lo, size = GATHER[sub]
        index = [slice(None)] * 3
        for later in range(phase, 3):
            index[order[later]] = place[order[later]]
        if phase:
            index[order[phase - 1]] = moved(order[phase - 1], unit_by)
        index[order[phase]] = where
        return tokens.at[(*index, slice(None), pl.ds(lo, size))]

    def slot(phase, unit_by):
        return 0 if phase == 0 else 4 * phase - 3 + unit_by % 4

    def ag_copy(phase, sub, unit_by, message, where, by):
        block = gathered(phase, sub, unit_by, where)
        return pltpu.make_async_remote_copy(
            src_ref=block, dst_ref=block,
            send_sem=ag_send.at[sub, slot(phase, unit_by), message],
            recv_sem=ag_recv.at[sub, slot(phase, unit_by), message],
            device_id=neighbour(GATHER[sub][0][phase], by), device_id_type=MESH,
        )

    def ag_start(phase, sub, unit_by=0):
        axis, way = GATHER[sub][0][phase], GATHER[sub][1]
        go(ag_copy(phase, sub, unit_by, 0, place[axis], way))
        go(ag_copy(phase, sub, unit_by, 1, place[axis], -way))

    def ag_forward(phase, sub, unit_by=0):
        axis, way = GATHER[sub][0][phase], GATHER[sub][1]
        ag_copy(phase, sub, unit_by, 0, moved(axis, -way), way).wait_recv()
        go(ag_copy(phase, sub, unit_by, 2, moved(axis, -way), way))

    def ag_wait(phase, sub, message, unit_by=0):
        axis, way = GATHER[sub][0][phase], GATHER[sub][1]
        ag_copy(phase, sub, unit_by, message, moved(axis, way if message == 1 else 2), way).wait_recv()

    def plane(order, where):
        index = [slice(None)] * 3
        index[order[2]] = where
        return tuple(index)

    def first_products(sub, by):
        order, way, lo, size = GATHER[sub]
        at = plane(order, moved(order[2], by))
        block = tokens[(*at, slice(None), pl.ds(lo, size))].reshape(256, size)
        above = jnp.dot(block, up[pl.ds(lo, size), :], preferred_element_type=jnp.float32)
        hid[(*at, pl.ds(0, 8), pl.ds(0, HID))] += above.reshape(4, 4, 16, HID)[:, :, :8]
        down = part[lo // HALF, :, :, :, pl.ds(lo % HALF, size)].reshape(HID, size)
        below = lax.dot_general(block, down, (((1,), (1,)), ((), ())), preferred_element_type=jnp.float32)
        hid[(*at, pl.ds(8, 8), pl.ds(HID, HID))] += below.reshape(4, 4, 16, HID)[:, :, 8:]

    def way_of(sub):
        return GATHER[sub][1]

    for sub in SUBS:
        ag_start(0, sub)
    for sub in SUBS:
        ag_start(1, sub, 0)
    load_up = pltpu.make_async_copy(up_hbm, up, load_sem.at[0])
    load_down = [
        pltpu.make_async_copy(down_hbm.at[:, :, :, pl.ds(half * HALF, HALF)], part.at[half], load_sem.at[1 + half])
        for half in range(2)
    ]
    load_up.start()
    for load in load_down:
        load.start()
    hid[...] = jnp.zeros_like(hid)
    for sub in SUBS:
        ag_forward(0, sub)
        ag_start(1, sub, -way_of(sub))
    for sub in SUBS:
        ag_wait(0, sub, 1)
        ag_start(1, sub, way_of(sub))
    for sub in SUBS:
        ag_forward(1, sub, 0)
    for sub in SUBS:
        ag_wait(0, sub, 2)
        ag_start(1, sub, 2)
        ag_start(2, sub, 0)
    for sub in SUBS:
        ag_forward(1, sub, -way_of(sub))
    for sub in SUBS:
        ag_forward(1, sub, way_of(sub))
    for sub in SUBS:
        ag_forward(1, sub, 2)
        ag_start(2, sub, -way_of(sub))
    for sub in SUBS:
        for unit_by in range(4):
            ag_wait(1, sub, 1, unit_by)
        ag_start(2, sub, way_of(sub))
    for sub in SUBS:
        for unit_by in range(4):
            ag_wait(1, sub, 2, unit_by)
        ag_start(2, sub, 2)
    load_up.wait()
    for load in load_down:
        load.wait()
    for sub in SUBS:
        ag_forward(2, sub, 0)
    for sub in SUBS:
        first_products(sub, 0)
    for sub in SUBS:
        ag_forward(2, sub, -way_of(sub))
    for sub in SUBS:
        ag_forward(2, sub, way_of(sub))
    for sub in SUBS:
        ag_forward(2, sub, 2)
    for sub in SUBS:
        first_products(sub, -way_of(sub))
    for sub in SUBS:
        for unit_by in range(4):
            ag_wait(2, sub, 1, unit_by)
        first_products(sub, way_of(sub))
    for sub in SUBS:
        for unit_by in range(4):
            ag_wait(2, sub, 2, unit_by)
        first_products(sub, 2)

    SWAPPED = (0, 2, 1, 3)

    def activate(step, carry):
        z, y = step // 4, step % 4
        act, derivative = gelu_pair(hid[z, y, :, 0:8, 0:HID])
        for x in range(4):
            hid[z, y, x, 0:8, HID:] = hid[y, z, SWAPPED[x], 8:16, HID:] * derivative[x]
            hid[z, y, x, 0:8, 0:HID] = act[x]
        return carry

    lax.fori_loop(0, 16, activate, 0)

    def lay_out(step, carry):
        z, y = step // 4, step % 4
        blank = jnp.zeros((8, HID), jnp.float32)
        for x in range(4):
            weights[z, y, x, :, 0:HID] = jnp.concatenate([hid[z, y, x, 0:8, HID:], blank], axis=0).astype(jnp.bfloat16)
            weights[z, y, x, :, HID:] = jnp.concatenate(
                [blank, hid[y, z, SWAPPED[x], 0:8, 0:HID]], axis=0
            ).astype(jnp.bfloat16)
        return carry

    def second_products(sub, by):
        order, _, lo, size = SCATTER[sub]
        at = plane(order, moved(order[2], by))
        left = hid[(*at, pl.ds(0, 8), pl.ds(HID, HID))].reshape(128, HID).astype(jnp.bfloat16)
        halves = []
        for start in (lo, HALF + lo):
            halves.append(
                lax.dot_general(
                    left, up[pl.ds(start, size), :], (((1,), (1,)), ((), ())), preferred_element_type=jnp.float32
                ).reshape(4, 4, 8, size)
            )
        part[(*at, slice(None), pl.ds(lo, size))] = jnp.concatenate(halves, axis=2).astype(jnp.bfloat16)

    def two_axes(order, b_index, a_index=slice(None)):
        return tuple(b_index if axis == order[1] else a_index for axis in range(3) if axis != order[2])

    def landing(phase, sub, unit_by, message):
        order, _, lo, size = SCATTER[sub]
        columns = (slice(None), pl.ds(lo, size))
        if phase == 0:
            return got0.at[(message, *two_axes(order, moved(order[1], unit_by)), *columns)]
        if phase == 1:
            return got1.at[(message, moved(order[0], unit_by), *columns)]
        return got2.at[(message, *columns)]

    def share(phase, sub, unit_by, by):
        order, _, lo, size = SCATTER[sub]
        columns = (slice(None), pl.ds(lo, size))
        where = moved(order[2 - phase], by)
        if phase == 0:
            index = list(plane(order, where))
            index[order[1]] = moved(order[1], unit_by)
            return part.at[(*index, *columns)]
        if phase == 1:
            return got0.at[(2, *two_axes(order, where, moved(order[0], unit_by)), *columns)]
        return got1.at[(2, where, *columns)]

    def rs_copy(phase, sub, unit_by, message):
        order, way = SCATTER[sub][0], SCATTER[sub][1]
        if message == 0:
            source, by = share(phase, sub, unit_by, 2), -way
        elif message == 1:
            source, by = share(phase, sub, unit_by, way), way
        else:
            source, by = landing(phase, sub, unit_by, 0), -way
        at = slot(2, unit_by) if phase == 0 else slot(1, unit_by) if phase == 1 else 0
        return pltpu.make_async_remote_copy(
            src_ref=source, dst_ref=landing(phase, sub, unit_by, message),
            send_sem=rs_send.at[sub, at, message], recv_sem=rs_recv.at[sub, at, message],
            device_id=neighbour(order[2 - phase], by), device_id_type=MESH,
        )

    def rs_start(phase, sub, unit_by, message):
        go(rs_copy(phase, sub, unit_by, message))

    def rs_forward(phase, sub, unit_by=0):
        rs_copy(phase, sub, unit_by, 0).wait_recv()
        ref = landing(phase, sub, unit_by, 0)
        mine = share(phase, sub, unit_by, -way_of(sub))
        ref[...] = (f32(ref[...]) + f32(mine[...])).astype(jnp.bfloat16)
        rs_start(phase, sub, unit_by, 2)

    def rs_sum(phase, sub, unit_by=0):
        rs_copy(phase, sub, unit_by, 1).wait_recv()
        rs_copy(phase, sub, unit_by, 2).wait_recv()
        mine = share(phase, sub, unit_by, 0)
        ref = landing(phase, sub, unit_by, 2)
        summed = f32(mine[...]) + f32(landing(phase, sub, unit_by, 1)[...]) + f32(ref[...])
        if phase < 2:
            ref[...] = summed.astype(jnp.bfloat16)
        return summed

    def far_first(sub):
        return (2, way_of(sub), -way_of(sub), 0)

    for sub in SUBS:
        second_products(sub, 2)
        for unit_by in far_first(sub):
            rs_start(0, sub, unit_by, 0)
    for sub in SUBS:
        second_products(sub, way_of(sub))
        for unit_by in far_first(sub):
            rs_start(0, sub, unit_by, 1)
    for sub in SUBS:
        second_products(sub, -way_of(sub))
    for turn in range(4):
        for sub in SUBS:
            rs_forward(0, sub, far_first(sub)[turn])
    for sub in SUBS:
        second_products(sub, 0)
    lax.fori_loop(0, 16, lay_out, 0)

    def gain_tile(step, carry):
        at = pl.ds(pl.multiple_of(step * 256, 256), 256)
        also = pl.ds(pl.multiple_of(HALF + step * 256, 256), 256)
        sums = [jnp.zeros((8, 256), jnp.float32)] * 2
        for z in range(4):
            here = f32(part[z, :, :, :, at]).reshape(16, 16, 256)
            for half, columns in enumerate((at, also)):
                rows = f32(tokens[z, :, :, :, columns]).reshape(16, 16, 256)[:, :8]
                sums[half] = sums[half] + jnp.sum(here[:, 8 * half : 8 * half + 8] * rows, axis=0)
        gain_acc[:, at] = sums[0]
        gain_acc[:, also] = sums[1]
        return carry

    lax.fori_loop(0, HALF // 256, gain_tile, 0)
    gain_slots[0, place[2]] = jnp.sum(gain_acc[...], axis=0, keepdims=True) / f32(gain[...])

    def gain_copy(phase, by, owner):
        axis = 2 - phase
        return pltpu.make_async_remote_copy(
            src_ref=gain_slots.at[phase, owner], dst_ref=gain_slots.at[phase, owner],
            send_sem=gain_send.at[phase, by - 1], recv_sem=gain_recv.at[phase, by - 1],
            device_id=neighbour(axis, by), device_id_type=MESH,
        )

    def gain_start(phase):
        for by in (1, 2, 3):
            go(gain_copy(phase, by, place[2 - phase]))

    def gain_sum(phase):
        for by in (1, 2, 3):
            gain_copy(phase, by, moved(2 - phase, -by)).wait_recv()
        return (gain_slots[phase, 0] + gain_slots[phase, 1]) + (gain_slots[phase, 2] + gain_slots[phase, 3])

    TILE = 512

    def weight_tile(step, carry):
        at = pl.ds(pl.multiple_of(step * TILE, TILE), TILE)
        block = tokens[:, :, :, :, at].reshape(1024, TILE)
        up_grad[at, :] = lax.dot_general(
            block, weights[:, :, :, :, 0:HID].reshape(1024, HID), (((0,), (0,)), ((), ())),
            preferred_element_type=jnp.float32,
        )
        down_grad[:, at] = lax.dot_general(
            weights[:, :, :, :, HID:].reshape(1024, HID), block, (((0,), (0,)), ((), ())),
            preferred_element_type=jnp.float32,
        )
        return carry

    gain_start(0)
    lax.fori_loop(0, 8, weight_tile, 0)
    gain_slots[1, place[1]] = gain_sum(0)
    gain_start(1)
    lax.fori_loop(8, 16, weight_tile, 0)
    gain_slots[2, place[0]] = gain_sum(1)
    gain_start(2)

    for sub in SUBS:
        rs_sum(0, sub, 2)
        for unit_by in far_first(sub):
            rs_start(1, sub, unit_by, 0)
    for sub in SUBS:
        rs_sum(0, sub, way_of(sub))
        for unit_by in far_first(sub):
            rs_start(1, sub, unit_by, 1)
    for sub in SUBS:
        rs_sum(0, sub, -way_of(sub))
    for turn in range(4):
        for sub in SUBS:
            rs_forward(1, sub, far_first(sub)[turn])
    for sub in SUBS:
        rs_sum(0, sub, 0)
    gain_grad[...] = gain_sum(2)
    for sub in SUBS:
        rs_sum(1, sub, 2)
        rs_start(2, sub, 0, 0)
    for sub in SUBS:
        rs_sum(1, sub, way_of(sub))
        rs_start(2, sub, 0, 1)
    for sub in SUBS:
        rs_sum(1, sub, -way_of(sub))
    for sub in SUBS:
        rs_forward(2, sub)
    for sub in SUBS:
        rs_sum(1, sub, 0)
    own[...] = f32(tokens[place[1], place[0], (place[2] % 2) * 2 + place[2] // 2])[8:]
    for sub in SUBS:
        _, _, lo, size = SCATTER[sub]
        summed = rs_sum(2, sub)
        total[:, pl.ds(lo, size)] = summed[:8]
        total[:, pl.ds(HALF + lo, size)] = summed[8:]
    for copy in started:
        copy.wait_send()


def finish(
    up_grad, down_grad, total, unit, inverse, own, gain_grad, gain,
    input_out, gain_out, up_out, down_out,
    input_rows, sem,
):
    PIECES = 4
    copies = [pltpu.make_async_copy(gain_grad, gain_out, sem.at[0])]
    for piece in range(PIECES):
        for which, (source, target) in enumerate(((up_grad, up_out), (down_grad, down_out))):
            size = source.shape[0] // PIECES
            at = pl.ds(piece * size, size)
            copies.append(pltpu.make_async_copy(source.at[at, :], target.at[at, :], sem.at[2 + 2 * piece + which]))
    for copy in copies:
        copy.start()

    scaled = total[...] * f32(gain[...])
    units = unit[...]
    inner_mean = jnp.mean(scaled, axis=-1, keepdims=True)
    proj_mean = jnp.mean(scaled * units, axis=-1, keepdims=True)
    change = inverse[:, 0:1] * (scaled - inner_mean - units * proj_mean)
    input_rows[...] = (own[...] + change).astype(jnp.bfloat16)
    copies.append(pltpu.make_async_copy(input_rows, input_out, sem.at[1]))
    copies[-1].start()
    for copy in copies:
        copy.wait()


def on_device(upstream, saved_input, norm_gain, up_weight, down_weight):
    bf16, f4 = jnp.bfloat16, jnp.float32
    vmem, hbm = pl.BlockSpec(memory_space=pltpu.VMEM), pl.BlockSpec(memory_space=pl.ANY)
    dma = pltpu.SemaphoreType.DMA
    held = pl.pallas_call(
        kernel,
        out_shape=[
            pltpu.VMEM((D, HID), f4),
            pltpu.VMEM((HID, D), f4),
            pltpu.VMEM((ROWS, D), f4),
            pltpu.VMEM((ROWS, D), f4),
            pltpu.VMEM((ROWS, 128), f4),
            pltpu.VMEM((ROWS, D), f4),
            pltpu.VMEM((1, D), f4),
        ],
        in_specs=[vmem, vmem, vmem, hbm, hbm],
        out_specs=[vmem] * 7,
        scratch_shapes=[
            pltpu.VMEM((4, 4, 4, 16, D), bf16),
            pltpu.VMEM((4, 4, 4, 16, 2 * HID), bf16),
            pltpu.VMEM((D, HID), bf16),
            pltpu.VMEM((4, 4, 4, 16, HALF), bf16),
            pltpu.VMEM((3, 4, 4, 16, HALF), bf16),
            pltpu.VMEM((3, 4, 16, HALF), bf16),
            pltpu.VMEM((3, 16, HALF), bf16),
            pltpu.VMEM((4, 4, 4, 16, 2 * HID), f4),
            pltpu.VMEM((ROWS, D), f4),
            pltpu.VMEM((ROWS, D), f4),
            pltpu.VMEM((ROWS, D), f4),
            pltpu.VMEM((3, 4, 1, D), f4),
            dma((3,)), dma((2,)),
            dma((6, 9, 3)), dma((6, 9, 3)), dma((6, 9, 3)), dma((6, 9, 3)),
            dma((3, 3)), dma((3, 3)),
        ],
        compiler_params=pltpu.CompilerParams(
            collective_id=0, has_side_effects=True, vmem_limit_bytes=42 * 2**20
        ),
        name="section_backward",
    )(upstream[0], saved_input[0], norm_gain, up_weight[0], down_weight[0].reshape(4, 4, 16, D))
    held = [pltpu.with_memory_space_constraint(array, pltpu.VMEM) for array in held]
    input_grad, gain_grad, up_grad, down_grad = pl.pallas_call(
        finish,
        out_shape=[
            jax.ShapeDtypeStruct((ROWS, D), bf16),
            jax.ShapeDtypeStruct((1, D), f4),
            jax.ShapeDtypeStruct((D, HID), f4),
            jax.ShapeDtypeStruct((HID, D), f4),
        ],
        in_specs=[vmem] * 8,
        out_specs=[hbm] * 4,
        scratch_shapes=[
            pltpu.VMEM((ROWS, D), bf16),
            dma((10,)),
        ],
        compiler_params=pltpu.CompilerParams(vmem_limit_bytes=4 * 2**20),
        name="finish",
    )(*held, norm_gain)
    return (input_grad[None], up_grad[None], down_grad[None], gain_grad)


def solution(mesh):
    in_specs = (
        P("section", ("dp", "tensor"), None),
        P("section", ("dp", "tensor"), None),
        P("section", None),
        P("section", None, ("dp", "tensor")),
        P("section", ("dp", "tensor"), None),
    )
    out_specs = (
        P("section", ("dp", "tensor"), None),
        P("section", None, ("dp", "tensor")),
        P("section", ("dp", "tensor"), None),
        P("section", None),
    )
    return jax.shard_map(
        on_device, mesh=mesh, in_specs=in_specs, out_specs=out_specs, check_vma=False
    )
```

time: 151 us -> 138 us (0.914)
  local copies, waits for them, and re-layouts: 13.2 us -> 0.01 us
    unnamed x10 -> x2, local copies, waits for them, and re-layouts: 13.2 us -> 0.01 us
    pallas_call x1 -> x2, Pallas kernels: 137 us -> 137 us  [the longest x1 131 us: on_device(): pl.pallas_call(kernel, out_shape=[pltpu.VMEM((D, HID), f4), pltpu.VMEM((H...]
where the time goes in v2:
time: 138 us
  Pallas kernels  137 us (99%)
    pallas_call x1, Pallas kernels, on_device(): pl.pallas_call(kernel, out_shape=[pltpu.VMEM((D, HID), f4), pltpu.VMEM((H...  131 us
    pallas_call x1, Pallas kernels, on_device(): pl.pallas_call(finish, out_shape=[jax.ShapeDtypeStruct((ROWS, D), bf16),...  5.96 us

profile of v2, /device:TPU:0, one launch (start us, length us, event | category | flops | bytes accessed | tf_op | source)
XLA Modules:
  0.0 137.6 jit_solution(13120810128321464801)
XLA Ops:
  0.6 0.0 copy-start
  0.6 130.9 %section_backward.1 = (f32[8192,256]{1,0:T(8,128)S(1)}, f32[256,8192]{1,0:T(8,128)S(1)}, f32[8,8192]{1,0:T(8,128)S(1)}, f32[8,8192]{1,0:T(8,128)S(1)}, f32[8,128...) custom-call(bf16[8,8192]{1,0:T(8,128)(2,1)} %bitcast.9, bf16[8,8192]{1,0:T(8,128)(2,1)} %bitcast.10, ...), custom_call_target="tpu_custom_call" | custom-call | tf_op jit(solution)/shard_map/section_backward/pallas_call | solution.py:453
  131.5 0.0 copy-done
  131.5 6.0 %finish.1 = (bf16[8,8192]{1,0:T(8,128)(2,1)}, f32[1,8192]{1,0:T(1,128)}, f32[8192,256]{1,0:T(8,128)}, f32[256,8192]{1,0:T(8,128)}) custom-call(f32[8192,256]{1,0:T(8,128)S(1)} %get-tuple-element.15.up_grad, f32[256,8192]{1,0:T(8,128)S(1)} %get-tuple-element.16.down_grad, f32[8,8192]{1,0:T(8,128)S(1)} %get-tuple-element.17.total, ...), custom_call_target="tpu_custom_call" | custom-call | tf_op jit(solution)/shard_map/finish/pallas_call | solution.py:489
Async XLA Ops:
  0.6 130.9 %copy-start = (bf16[1,8192]{1,0:T(2,128)(2,1)S(1)}, bf16[1,8192]{1,0:T(2,128)(2,1)}, u32[]{:S(2)}) copy-start(bf16[1,8192]{1,0:T(2,128)(2,1)} %gain.3) | copy-start | bytes 49156

commit v3 on v2

--- a/solution.py
+++ b/solution.py
@@ -41,6 +41,11 @@
 
 def f32(value):
     return value.astype(jnp.float32)
+
+
+def apart(blocks, size):
+    wide = f32(blocks).reshape(-1, 16, size)
+    return tuple(half.reshape(-1, size).astype(jnp.bfloat16) for half in (wide[:, :8], wide[:, 8:]))
 
 
 def kernel(
@@ -137,12 +142,12 @@
     def first_products(sub, by):
         order, way, lo, size = GATHER[sub]
         at = plane(order, moved(order[2], by))
-        block = tokens[(*at, slice(None), pl.ds(lo, size))].reshape(256, size)
-        above = jnp.dot(block, up[pl.ds(lo, size), :], preferred_element_type=jnp.float32)
-        hid[(*at, pl.ds(0, 8), pl.ds(0, HID))] += above.reshape(4, 4, 16, HID)[:, :, :8]
+        above, below = apart(tokens[(*at, slice(None), pl.ds(lo, size))], size)
+        above = jnp.dot(above, up[pl.ds(lo, size), :], preferred_element_type=jnp.float32)
+        hid[(*at, pl.ds(0, 8), pl.ds(0, HID))] += above.reshape(4, 4, 8, HID)
         down = part[lo // HALF, :, :, :, pl.ds(lo % HALF, size)].reshape(HID, size)
-        below = lax.dot_general(block, down, (((1,), (1,)), ((), ())), preferred_element_type=jnp.float32)
-        hid[(*at, pl.ds(8, 8), pl.ds(HID, HID))] += below.reshape(4, 4, 16, HID)[:, :, 8:]
+        below = lax.dot_general(below, down, (((1,), (1,)), ((), ())), preferred_element_type=jnp.float32)
+        hid[(*at, pl.ds(8, 8), pl.ds(HID, HID))] += below.reshape(4, 4, 8, HID)
 
     def way_of(sub):
         return GATHER[sub][1]
@@ -225,11 +230,13 @@
 
     def lay_out(step, carry):
         z, y = step // 4, step % 4
-        blank = jnp.zeros((8, HID), jnp.float32)
-        for x in range(4):
-            weights[z, y, x, :, 0:HID] = jnp.concatenate([hid[z, y, x, 0:8, HID:], blank], axis=0).astype(jnp.bfloat16)
-            weights[z, y, x, :, HID:] = jnp.concatenate(
-                [blank, hid[y, z, SWAPPED[x], 0:8, 0:HID]], axis=0
+        for pair in range(2):
+            first, second = 2 * pair, 2 * pair + 1
+            weights[0, z, y, pair] = jnp.concatenate(
+                [hid[z, y, x, 0:8, HID:] for x in (first, second)], axis=0
+            ).astype(jnp.bfloat16)
+            weights[1, z, y, pair] = jnp.concatenate(
+                [hid[y, z, SWAPPED[x], 0:8, 0:HID] for x in (first, second)], axis=0
             ).astype(jnp.bfloat16)
         return carry
 
@@ -310,20 +317,36 @@
 
     for sub in SUBS:
         second_products(sub, 2)
-        for unit_by in far_first(sub):
-            rs_start(0, sub, unit_by, 0)
+        for turn in (0, 1):
+            rs_start(0, sub, far_first(sub)[turn], 0)
     for sub in SUBS:
         second_products(sub, way_of(sub))
-        for unit_by in far_first(sub):
-            rs_start(0, sub, unit_by, 1)
+        rs_start(0, sub, far_first(sub)[0], 1)
     for sub in SUBS:
         second_products(sub, -way_of(sub))
-    for turn in range(4):
+
+    def line_step(turn):
         for sub in SUBS:
             rs_forward(0, sub, far_first(sub)[turn])
+            if turn < 2:
+                rs_start(0, sub, far_first(sub)[turn + 2], 0)
+            if turn < 3:
+                rs_start(0, sub, far_first(sub)[turn + 1], 1)
+
+    def line_sum(turn):
+        for sub in SUBS:
+            rs_sum(0, sub, far_first(sub)[turn])
+            if turn < 2:
+                for unit_by in far_first(sub):
+                    rs_start(1, sub, unit_by, turn)
+
+    line_step(0)
+    lax.fori_loop(0, 16, lay_out, 0)
+    line_step(1)
     for sub in SUBS:
         second_products(sub, 0)
-    lax.fori_loop(0, 16, lay_out, 0)
+    line_sum(0)
+    line_step(2)
 
     def gain_tile(step, carry):
         at = pl.ds(pl.multiple_of(step * 256, 256), 256)
@@ -362,53 +385,41 @@
 
     def weight_tile(step, carry):
         at = pl.ds(pl.multiple_of(step * TILE, TILE), TILE)
-        block = tokens[:, :, :, :, at].reshape(1024, TILE)
+        above, below = apart(tokens[:, :, :, :, at], TILE)
         up_grad[at, :] = lax.dot_general(
-            block, weights[:, :, :, :, 0:HID].reshape(1024, HID), (((0,), (0,)), ((), ())),
-            preferred_element_type=jnp.float32,
+            above, weights[0].reshape(512, HID), (((0,), (0,)), ((), ())), preferred_element_type=jnp.float32
         )
         down_grad[:, at] = lax.dot_general(
-            weights[:, :, :, :, HID:].reshape(1024, HID), block, (((0,), (0,)), ((), ())),
-            preferred_element_type=jnp.float32,
+            weights[1].reshape(512, HID), below, (((0,), (0,)), ((), ())), preferred_element_type=jnp.float32
         )
         return carry
 
     gain_start(0)
-    lax.fori_loop(0, 8, weight_tile, 0)
+    line_sum(1)
+    line_step(3)
+    lax.fori_loop(0, 6, weight_tile, 0)
     gain_slots[1, place[1]] = gain_sum(0)
     gain_start(1)
-    lax.fori_loop(8, 16, weight_tile, 0)
-    gain_slots[2, place[0]] = gain_sum(1)
-    gain_start(2)
-
-    for sub in SUBS:
-        rs_sum(0, sub, 2)
-        for unit_by in far_first(sub):
-            rs_start(1, sub, unit_by, 0)
-    for sub in SUBS:
-        rs_sum(0, sub, way_of(sub))
-        for unit_by in far_first(sub):
-            rs_start(1, sub, unit_by, 1)
-    for sub in SUBS:
-        rs_sum(0, sub, -way_of(sub))
+    line_sum(2)
     for turn in range(4):
         for sub in SUBS:
             rs_forward(1, sub, far_first(sub)[turn])
-    for sub in SUBS:
-        rs_sum(0, sub, 0)
+    lax.fori_loop(6, 12, weight_tile, 0)
+    gain_slots[2, place[0]] = gain_sum(1)
+    gain_start(2)
+    line_sum(3)
+    for turn in (0, 1):
+        for sub in SUBS:
+            rs_sum(1, sub, far_first(sub)[turn])
+            rs_start(2, sub, 0, turn)
+    lax.fori_loop(12, 16, weight_tile, 0)
+    for sub in SUBS:
+        rs_sum(1, sub, -way_of(sub))
+    for sub in SUBS:
+        rs_forward(2, sub)
+    for sub in SUBS:
+        rs_sum(1, sub, 0)
     gain_grad[...] = gain_sum(2)
-    for sub in SUBS:
-        rs_sum(1, sub, 2)
-        rs_start(2, sub, 0, 0)
-    for sub in SUBS:
-        rs_sum(1, sub, way_of(sub))
-        rs_start(2, sub, 0, 1)
-    for sub in SUBS:
-        rs_sum(1, sub, -way_of(sub))
-    for sub in SUBS:
-        rs_forward(2, sub)
-    for sub in SUBS:
-        rs_sum(1, sub, 0)
     own[...] = f32(tokens[place[1], place[0], (place[2] % 2) * 2 + place[2] // 2])[8:]
     for sub in SUBS:
         _, _, lo, size = SCATTER[sub]
@@ -465,7 +476,7 @@
         out_specs=[vmem] * 7,
         scratch_shapes=[
             pltpu.VMEM((4, 4, 4, 16, D), bf16),
-            pltpu.VMEM((4, 4, 4, 16, 2 * HID), bf16),
+            pltpu.VMEM((2, 4, 4, 2, 16, HID), bf16),
             pltpu.VMEM((D, HID), bf16),
             pltpu.VMEM((4, 4, 4, 16, HALF), bf16),
             pltpu.VMEM((3, 4, 4, 16, HALF), bf16),

time: 138 us -> 131 us (0.949)
  Pallas kernels: 137 us -> 130 us
    pallas_call x1, Pallas kernels: 131 us -> 124 us  [on_device(): pl.pallas_call(kernel, out_shape=[pltpu.VMEM((D, HID), f4), pltpu.VMEM((H...]
where the time goes in v3:
time: 131 us
  Pallas kernels  130 us (99%)
    pallas_call x1, Pallas kernels, on_device(): pl.pallas_call(kernel, out_shape=[pltpu.VMEM((D, HID), f4), pltpu.VMEM((H...  124 us
    pallas_call x1, Pallas kernels, on_device(): pl.pallas_call(finish, out_shape=[jax.ShapeDtypeStruct((ROWS, D), bf16),...  5.96 us

profile of v3, /device:TPU:0, one launch (start us, length us, event | category | flops | bytes accessed | tf_op | source)
XLA Modules:
  0.0 130.7 jit_solution(12286361276514795641)
XLA Ops:
  0.6 0.0 copy-start
  0.6 123.9 %section_backward.1 = (f32[8192,256]{1,0:T(8,128)S(1)}, f32[256,8192]{1,0:T(8,128)S(1)}, f32[8,8192]{1,0:T(8,128)S(1)}, f32[8,8192]{1,0:T(8,128)S(1)}, f32[8,128...) custom-call(bf16[8,8192]{1,0:T(8,128)(2,1)} %bitcast.9, bf16[8,8192]{1,0:T(8,128)(2,1)} %bitcast.10, ...), custom_call_target="tpu_custom_call" | custom-call | tf_op jit(solution)/shard_map/section_backward/pallas_call | solution.py:464
  124.5 0.0 copy-done
  124.6 6.0 %finish.1 = (bf16[8,8192]{1,0:T(8,128)(2,1)}, f32[1,8192]{1,0:T(1,128)}, f32[8192,256]{1,0:T(8,128)}, f32[256,8192]{1,0:T(8,128)}) custom-call(f32[8192,256]{1,0:T(8,128)S(1)} %get-tuple-element.15.up_grad, f32[256,8192]{1,0:T(8,128)S(1)} %get-tuple-element.16.down_grad, f32[8,8192]{1,0:T(8,128)S(1)} %get-tuple-element.17.total, ...), custom_call_target="tpu_custom_call" | custom-call | tf_op jit(solution)/shard_map/finish/pallas_call | solution.py:500
Async XLA Ops:
  0.6 123.9 %copy-start = (bf16[1,8192]{1,0:T(2,128)(2,1)S(1)}, bf16[1,8192]{1,0:T(2,128)(2,1)}, u32[]{:S(2)}) copy-start(bf16[1,8192]{1,0:T(2,128)(2,1)} %gain.3) | copy-start | bytes 49156

commit v4 on v3

--- a/solution.py
+++ b/solution.py
@@ -139,15 +139,36 @@
         index[order[2]] = where
         return tuple(index)
 
-    def first_products(sub, by):
-        order, way, lo, size = GATHER[sub]
-        at = plane(order, moved(order[2], by))
-        above, below = apart(tokens[(*at, slice(None), pl.ds(lo, size))], size)
+    def first_products(number, by, lines=None):
+        subs = (2 * number, 2 * number + 1)
+        order, _, lo, _ = GATHER[subs[0]]
+        size = GATHER[subs[0]][3] + GATHER[subs[1]][3]
+        places = []
+        for line in (None,) if lines is None else lines:
+            at = list(plane(order, moved(order[2], by)))
+            if line is not None:
+                at[order[1]] = moved(order[1], line)
+            places.append(tuple(at))
+        blocks = [tokens[(*at, slice(None), pl.ds(lo, size))].reshape(-1, 16, size) for at in places]
+        above, below = apart(blocks[0] if len(blocks) == 1 else jnp.concatenate(blocks, axis=0), size)
         above = jnp.dot(above, up[pl.ds(lo, size), :], preferred_element_type=jnp.float32)
-        hid[(*at, pl.ds(0, 8), pl.ds(0, HID))] += above.reshape(4, 4, 8, HID)
-        down = part[lo // HALF, :, :, :, pl.ds(lo % HALF, size)].reshape(HID, size)
-        below = lax.dot_general(below, down, (((1,), (1,)), ((), ())), preferred_element_type=jnp.float32)
-        hid[(*at, pl.ds(8, 8), pl.ds(HID, HID))] += below.reshape(4, 4, 8, HID)
+        sums = []
+        for sub in subs:
+            start, width = GATHER[sub][2], GATHER[sub][3]
+            down = part[start // HALF, :, :, :, pl.ds(start % HALF, width)].reshape(HID, width)
+            sums.append(
+                lax.dot_general(
+                    below[:, start - lo : start - lo + width], down, (((1,), (1,)), ((), ())),
+                    preferred_element_type=jnp.float32,
+                )
+            )
+        below = sums[0] + sums[1]
+        rows = above.shape[0] // len(places)
+        shape = ((4, 4) if lines is None else (4,)) + (8, HID)
+        for turn, at in enumerate(places):
+            some = slice(turn * rows, (turn + 1) * rows)
+            hid[(*at, pl.ds(0, 8), pl.ds(0, HID))] += above[some].reshape(shape)
+            hid[(*at, pl.ds(8, 8), pl.ds(HID, HID))] += below[some].reshape(shape)
 
     def way_of(sub):
         return GATHER[sub][1]
@@ -197,24 +218,29 @@
         load.wait()
     for sub in SUBS:
         ag_forward(2, sub, 0)
-    for sub in SUBS:
-        first_products(sub, 0)
+    for number in range(3):
+        first_products(number, 0)
     for sub in SUBS:
         ag_forward(2, sub, -way_of(sub))
     for sub in SUBS:
         ag_forward(2, sub, way_of(sub))
     for sub in SUBS:
         ag_forward(2, sub, 2)
-    for sub in SUBS:
-        first_products(sub, -way_of(sub))
-    for sub in SUBS:
-        for unit_by in range(4):
-            ag_wait(2, sub, 1, unit_by)
-        first_products(sub, way_of(sub))
-    for sub in SUBS:
-        for unit_by in range(4):
+    for number in range(3):
+        for sub in (2 * number, 2 * number + 1):
+            for unit_by in range(4):
+                ag_wait(2, sub, 1, unit_by)
+        first_products(number, 1)
+        first_products(number, -1)
+    for unit_by in (0, 1, 3):
+        for sub in SUBS:
             ag_wait(2, sub, 2, unit_by)
-        first_products(sub, 2)
+    for number in range(3):
+        first_products(number, 2, (0, 1, -1))
+    for number in range(3):
+        for sub in (2 * number, 2 * number + 1):
+            ag_wait(2, sub, 2, 2)
+        first_products(number, 2, (2,))
 
     SWAPPED = (0, 2, 1, 3)
 
@@ -261,9 +287,7 @@
         columns = (slice(None), pl.ds(lo, size))
         if phase == 0:
             return got0.at[(message, *two_axes(order, moved(order[1], unit_by)), *columns)]
-        if phase == 1:
-            return got1.at[(message, moved(order[0], unit_by), *columns)]
-        return got2.at[(message, *columns)]
+        return got1.at[(message, moved(order[0], unit_by), *columns)]
 
     def share(phase, sub, unit_by, by):
         order, _, lo, size = SCATTER[sub]
@@ -273,9 +297,7 @@
             index = list(plane(order, where))
             index[order[1]] = moved(order[1], unit_by)
             return part.at[(*index, *columns)]
-        if phase == 1:
-            return got0.at[(2, *two_axes(order, where, moved(order[0], unit_by)), *columns)]
-        return got1.at[(2, where, *columns)]
+        return got0.at[(2, *two_axes(order, where, moved(order[0], unit_by)), *columns)]
 
     def rs_copy(phase, sub, unit_by, message):
         order, way = SCATTER[sub][0], SCATTER[sub][1]
@@ -285,7 +307,7 @@
             source, by = share(phase, sub, unit_by, way), way
         else:
             source, by = landing(phase, sub, unit_by, 0), -way
-        at = slot(2, unit_by) if phase == 0 else slot(1, unit_by) if phase == 1 else 0
+        at = slot(2 - phase, unit_by)
         return pltpu.make_async_remote_copy(
             src_ref=source, dst_ref=landing(phase, sub, unit_by, message),
             send_sem=rs_send.at[sub, at, message], recv_sem=rs_recv.at[sub, at, message],
@@ -308,9 +330,16 @@
         mine = share(phase, sub, unit_by, 0)
         ref = landing(phase, sub, unit_by, 2)
         summed = f32(mine[...]) + f32(landing(phase, sub, unit_by, 1)[...]) + f32(ref[...])
-        if phase < 2:
-            ref[...] = summed.astype(jnp.bfloat16)
-        return summed
+        ref[...] = summed.astype(jnp.bfloat16)
+
+    def last_copy(sub, by):
+        order, _, lo, size = SCATTER[sub]
+        columns = (slice(None), pl.ds(lo, size))
+        return pltpu.make_async_remote_copy(
+            src_ref=got1.at[(2, moved(order[0], by), *columns)], dst_ref=got2.at[(by - 1, *columns)],
+            send_sem=rs_send.at[sub, 0, by - 1], recv_sem=rs_recv.at[sub, 0, by - 1],
+            device_id=neighbour(order[0], by), device_id_type=MESH,
+        )
 
     def far_first(sub):
         return (2, way_of(sub), -way_of(sub), 0)
@@ -321,7 +350,8 @@
             rs_start(0, sub, far_first(sub)[turn], 0)
     for sub in SUBS:
         second_products(sub, way_of(sub))
-        rs_start(0, sub, far_first(sub)[0], 1)
+        for turn in (0, 1):
+            rs_start(0, sub, far_first(sub)[turn], 1)
     for sub in SUBS:
         second_products(sub, -way_of(sub))
 
@@ -330,7 +360,7 @@
             rs_forward(0, sub, far_first(sub)[turn])
             if turn < 2:
                 rs_start(0, sub, far_first(sub)[turn + 2], 0)
-            if turn < 3:
+            if 0 < turn < 3:
                 rs_start(0, sub, far_first(sub)[turn + 1], 1)
 
     def line_sum(turn):
@@ -404,26 +434,28 @@
     for turn in range(4):
         for sub in SUBS:
             rs_forward(1, sub, far_first(sub)[turn])
-    lax.fori_loop(6, 12, weight_tile, 0)
+    lax.fori_loop(6, 13, weight_tile, 0)
     gain_slots[2, place[0]] = gain_sum(1)
     gain_start(2)
     line_sum(3)
-    for turn in (0, 1):
+    for turn in range(3):
         for sub in SUBS:
-            rs_sum(1, sub, far_first(sub)[turn])
-            rs_start(2, sub, 0, turn)
-    lax.fori_loop(12, 16, weight_tile, 0)
-    for sub in SUBS:
-        rs_sum(1, sub, -way_of(sub))
-    for sub in SUBS:
-        rs_forward(2, sub)
+            unit_by = far_first(sub)[turn]
+            rs_sum(1, sub, unit_by)
+            go(last_copy(sub, unit_by % 4))
     for sub in SUBS:
         rs_sum(1, sub, 0)
+    lax.fori_loop(13, 16, weight_tile, 0)
     gain_grad[...] = gain_sum(2)
     own[...] = f32(tokens[place[1], place[0], (place[2] % 2) * 2 + place[2] // 2])[8:]
     for sub in SUBS:
         _, _, lo, size = SCATTER[sub]
-        summed = rs_sum(2, sub)
+        for by in (1, 2, 3):
+            last_copy(sub, by).wait_recv()
+        columns = (slice(None), pl.ds(lo, size))
+        summed = f32(got1[(2, place[SCATTER[sub][0][0]], *columns)])
+        for by in (1, 2, 3):
+            summed = summed + f32(got2[(by - 1, *columns)])
         total[:, pl.ds(lo, size)] = summed[:8]
         total[:, pl.ds(HALF + lo, size)] = summed[8:]
     for copy in started:

time: 131 us -> 128 us (0.977)
  Pallas kernels: 130 us -> 127 us
    pallas_call x1, Pallas kernels: 124 us -> 121 us  [on_device(): pl.pallas_call(kernel, out_shape=[pltpu.VMEM((D, HID), f4), pltpu.VMEM((H...]
where the time goes in v4:
time: 128 us
  Pallas kernels  127 us (99%)
    pallas_call x1, Pallas kernels, on_device(): pl.pallas_call(kernel, out_shape=[pltpu.VMEM((D, HID), f4), pltpu.VMEM((H...  121 us
    pallas_call x1, Pallas kernels, on_device(): pl.pallas_call(finish, out_shape=[jax.ShapeDtypeStruct((ROWS, D), bf16),...  5.96 us

profile of v4, /device:TPU:0, one launch (start us, length us, event | category | flops | bytes accessed | tf_op | source)
XLA Modules:
  0.0 128.0 jit_solution(226225091986587810)
XLA Ops:
  0.6 0.0 copy-start
  0.6 121.2 %section_backward.1 = (f32[8192,256]{1,0:T(8,128)S(1)}, f32[256,8192]{1,0:T(8,128)S(1)}, f32[8,8192]{1,0:T(8,128)S(1)}, f32[8,8192]{1,0:T(8,128)S(1)}, f32[8,128...) custom-call(bf16[8,8192]{1,0:T(8,128)(2,1)} %bitcast.9, bf16[8,8192]{1,0:T(8,128)(2,1)} %bitcast.10, ...), custom_call_target="tpu_custom_call" | custom-call | tf_op jit(solution)/shard_map/section_backward/pallas_call | solution.py:496
  121.9 0.0 copy-done
  121.9 6.0 %finish.1 = (bf16[8,8192]{1,0:T(8,128)(2,1)}, f32[1,8192]{1,0:T(1,128)}, f32[8192,256]{1,0:T(8,128)}, f32[256,8192]{1,0:T(8,128)}) custom-call(f32[8192,256]{1,0:T(8,128)S(1)} %get-tuple-element.15.up_grad, f32[256,8192]{1,0:T(8,128)S(1)} %get-tuple-element.16.down_grad, f32[8,8192]{1,0:T(8,128)S(1)} %get-tuple-element.17.total, ...), custom_call_target="tpu_custom_call" | custom-call | tf_op jit(solution)/shard_map/finish/pallas_call | solution.py:532
Async XLA Ops:
  0.6 121.2 %copy-start = (bf16[1,8192]{1,0:T(2,128)(2,1)S(1)}, bf16[1,8192]{1,0:T(2,128)(2,1)}, u32[]{:S(2)}) copy-start(bf16[1,8192]{1,0:T(2,128)(2,1)} %gain.3) | copy-start | bytes 49156

commit v5 on v4

--- a/solution.py
+++ b/solution.py
@@ -17,17 +17,17 @@
 ORDERS = ((2, 1, 0), (0, 2, 1), (1, 0, 2))
 
 
-def cut(tiles):
-    subs, at = [], 0
-    for number, count in enumerate(tiles):
-        subs.append((ORDERS[number // 2], 1 if number % 2 == 0 else -1, at * 128, count * 128))
-        at += count
-    return tuple(subs)
-
-
-GATHER = cut((11, 11, 10, 11, 11, 10))
-SCATTER = cut((6, 5, 6, 5, 5, 5))
+def cut(pieces):
+    return tuple(
+        (ORDERS[number // 2], 1 if number % 2 == 0 else -1, at * 128, count * 128)
+        for number, (at, count) in enumerate(pieces)
+    )
+
+
+GATHER = cut(((0, 11), (32, 11), (11, 11), (43, 10), (22, 10), (53, 11)))
+SCATTER = cut(((0, 6), (6, 5), (11, 6), (17, 5), (22, 5), (27, 5)))
 SUBS = range(6)
+TURNS = (0, 2, 4, 1, 3, 5)
 
 
 def gelu_pair(hidden):
@@ -43,6 +43,10 @@
     return value.astype(jnp.float32)
 
 
+def folded(rows):
+    return jnp.concatenate([rows[:, :HALF], rows[:, HALF:]], axis=0)
+
+
 def apart(blocks, size):
     wide = f32(blocks).reshape(-1, 16, size)
     return tuple(half.reshape(-1, size).astype(jnp.bfloat16) for half in (wide[:, :8], wide[:, 8:]))
@@ -51,7 +55,7 @@
 def kernel(
     upstream, saved, gain, up_hbm, down_hbm,
     up_grad, down_grad, total, unit, inverse, own, gain_grad,
-    tokens, weights, up, part, got0, got1, got2, hid, sent_rows, arrived_rows, gain_acc, gain_slots,
+    tokens, weights, up, part, got0, got1, got2, hid, sent_rows, gain_acc, gain_slots,
     load_sem, swap_sem, ag_send, ag_recv, rs_send, rs_recv, gain_send, gain_recv,
 ):
     section = lax.axis_index("section")
@@ -81,22 +85,20 @@
     others = [neighbour(axis, by) for axis in range(3) for by in (1, 2, 3)] + [partner]
     for other in others:
         pl.semaphore_signal(barrier, inc=1, device_id=other, device_id_type=MESH)
-    sent_rows[...] = f32(upstream[...])
+    sent_rows[...] = folded(f32(upstream[...])).astype(jnp.bfloat16)
     rows = f32(saved[...])
     centered = rows - jnp.mean(rows, axis=-1, keepdims=True)
     spread = lax.rsqrt(jnp.mean(centered * centered, axis=-1, keepdims=True) + 1e-05)
     inverse[...] = jnp.broadcast_to(spread, inverse.shape)
     unit[...] = centered * spread
+    tokens[place[0], place[1], place[2], :, 0:HALF] = folded(unit[...] * f32(gain[...])).astype(jnp.bfloat16)
     pl.semaphore_wait(barrier, len(others))
 
     swap = pltpu.make_async_remote_copy(
-        src_ref=sent_rows, dst_ref=arrived_rows, send_sem=swap_sem.at[0], recv_sem=swap_sem.at[1],
-        device_id=partner, device_id_type=MESH,
+        src_ref=sent_rows, dst_ref=tokens.at[place[0], place[1], place[2], :, pl.ds(HALF, HALF)],
+        send_sem=swap_sem.at[0], recv_sem=swap_sem.at[1], device_id=partner, device_id_type=MESH,
     )
     go(swap)
-    normed = unit[...] * f32(gain[...])
-    swap.wait_recv()
-    tokens[place[0], place[1], place[2]] = jnp.concatenate([normed, arrived_rows[...]], axis=0).astype(jnp.bfloat16)
 
     def gathered(phase, sub, unit_by, where):
         order, _, lo, size = GATHER[sub]
@@ -139,10 +141,8 @@
         index[order[2]] = where
         return tuple(index)
 
-    def first_products(number, by, lines=None):
-        subs = (2 * number, 2 * number + 1)
-        order, _, lo, _ = GATHER[subs[0]]
-        size = GATHER[subs[0]][3] + GATHER[subs[1]][3]
+    def first_products(sub, by, lines=None):
+        order, _, lo, size = GATHER[sub]
         places = []
         for line in (None,) if lines is None else lines:
             at = list(plane(order, moved(order[2], by)))
@@ -150,33 +150,32 @@
                 at[order[1]] = moved(order[1], line)
             places.append(tuple(at))
         blocks = [tokens[(*at, slice(None), pl.ds(lo, size))].reshape(-1, 16, size) for at in places]
-        above, below = apart(blocks[0] if len(blocks) == 1 else jnp.concatenate(blocks, axis=0), size)
-        above = jnp.dot(above, up[pl.ds(lo, size), :], preferred_element_type=jnp.float32)
-        sums = []
-        for sub in subs:
-            start, width = GATHER[sub][2], GATHER[sub][3]
-            down = part[start // HALF, :, :, :, pl.ds(start % HALF, width)].reshape(HID, width)
-            sums.append(
-                lax.dot_general(
-                    below[:, start - lo : start - lo + width], down, (((1,), (1,)), ((), ())),
-                    preferred_element_type=jnp.float32,
-                )
-            )
-        below = sums[0] + sums[1]
-        rows = above.shape[0] // len(places)
+        halves = apart(blocks[0] if len(blocks) == 1 else jnp.concatenate(blocks, axis=0), size)
+        products = []
+        for half, rows in enumerate(halves):
+            if sub % 2 == 0:
+                matrix, dims = up[pl.ds(half * HALF + lo, size), :], (((1,), (0,)), ((), ()))
+            else:
+                matrix = part[half, :, :, :, pl.ds(lo - HALF, size)].reshape(HID, size)
+                dims = (((1,), (1,)), ((), ()))
+            products.append(lax.dot_general(rows, matrix, dims, preferred_element_type=jnp.float32))
+        summed = products[0] + products[1]
+        count = summed.shape[0] // len(places)
         shape = ((4, 4) if lines is None else (4,)) + (8, HID)
+        corner = (pl.ds(0, 8), pl.ds(0, HID)) if sub % 2 == 0 else (pl.ds(8, 8), pl.ds(HID, HID))
         for turn, at in enumerate(places):
-            some = slice(turn * rows, (turn + 1) * rows)
-            hid[(*at, pl.ds(0, 8), pl.ds(0, HID))] += above[some].reshape(shape)
-            hid[(*at, pl.ds(8, 8), pl.ds(HID, HID))] += below[some].reshape(shape)
+            hid[(*at, *corner)] += summed[turn * count : (turn + 1) * count].reshape(shape)
 
     def way_of(sub):
         return GATHER[sub][1]
 
-    for sub in SUBS:
-        ag_start(0, sub)
-    for sub in SUBS:
-        ag_start(1, sub, 0)
+    for half in range(2):
+        if half:
+            swap.wait_recv()
+        for sub in SUBS[half::2]:
+            ag_start(0, sub)
+        for sub in SUBS[half::2]:
+            ag_start(1, sub, 0)
     load_up = pltpu.make_async_copy(up_hbm, up, load_sem.at[0])
     load_down = [
         pltpu.make_async_copy(down_hbm.at[:, :, :, pl.ds(half * HALF, HALF)], part.at[half], load_sem.at[1 + half])
@@ -186,61 +185,60 @@
     for load in load_down:
         load.start()
     hid[...] = jnp.zeros_like(hid)
-    for sub in SUBS:
+    for sub in TURNS:
         ag_forward(0, sub)
         ag_start(1, sub, -way_of(sub))
-    for sub in SUBS:
+    for sub in TURNS:
         ag_wait(0, sub, 1)
         ag_start(1, sub, way_of(sub))
-    for sub in SUBS:
+    for sub in TURNS:
         ag_forward(1, sub, 0)
-    for sub in SUBS:
+    for sub in TURNS:
         ag_wait(0, sub, 2)
         ag_start(1, sub, 2)
         ag_start(2, sub, 0)
-    for sub in SUBS:
+    for sub in TURNS:
         ag_forward(1, sub, -way_of(sub))
-    for sub in SUBS:
+    for sub in TURNS:
         ag_forward(1, sub, way_of(sub))
-    for sub in SUBS:
+    for sub in TURNS:
         ag_forward(1, sub, 2)
         ag_start(2, sub, -way_of(sub))
-    for sub in SUBS:
+    for sub in TURNS:
         for unit_by in range(4):
             ag_wait(1, sub, 1, unit_by)
         ag_start(2, sub, way_of(sub))
-    for sub in SUBS:
+    for sub in TURNS:
         for unit_by in range(4):
             ag_wait(1, sub, 2, unit_by)
         ag_start(2, sub, 2)
     load_up.wait()
     for load in load_down:
         load.wait()
-    for sub in SUBS:
+    for sub in TURNS:
         ag_forward(2, sub, 0)
-    for number in range(3):
-        first_products(number, 0)
-    for sub in SUBS:
+    for sub in TURNS:
+        first_products(sub, 0)
+    for sub in TURNS:
         ag_forward(2, sub, -way_of(sub))
-    for sub in SUBS:
+    for sub in TURNS:
         ag_forward(2, sub, way_of(sub))
-    for sub in SUBS:
+    for sub in TURNS:
         ag_forward(2, sub, 2)
-    for number in range(3):
-        for sub in (2 * number, 2 * number + 1):
-            for unit_by in range(4):
-                ag_wait(2, sub, 1, unit_by)
-        first_products(number, 1)
-        first_products(number, -1)
+    for sub in TURNS:
+        first_products(sub, -way_of(sub))
+    for sub in TURNS:
+        for unit_by in range(4):
+            ag_wait(2, sub, 1, unit_by)
+        first_products(sub, way_of(sub))
     for unit_by in (0, 1, 3):
-        for sub in SUBS:
+        for sub in TURNS:
             ag_wait(2, sub, 2, unit_by)
-    for number in range(3):
-        first_products(number, 2, (0, 1, -1))
-    for number in range(3):
-        for sub in (2 * number, 2 * number + 1):
-            ag_wait(2, sub, 2, 2)
-        first_products(number, 2, (2,))
+    for sub in TURNS:
+        first_products(sub, 2, (0, 1, -1))
+    for sub in TURNS:
+        ag_wait(2, sub, 2, 2)
+        first_products(sub, 2, (2,))
 
     SWAPPED = (0, 2, 1, 3)
 
@@ -381,14 +379,11 @@
     def gain_tile(step, carry):
         at = pl.ds(pl.multiple_of(step * 256, 256), 256)
         also = pl.ds(pl.multiple_of(HALF + step * 256, 256), 256)
-        sums = [jnp.zeros((8, 256), jnp.float32)] * 2
+        sums = jnp.zeros((16, 256), jnp.float32)
         for z in range(4):
-            here = f32(part[z, :, :, :, at]).reshape(16, 16, 256)
-            for half, columns in enumerate((at, also)):
-                rows = f32(tokens[z, :, :, :, columns]).reshape(16, 16, 256)[:, :8]
-                sums[half] = sums[half] + jnp.sum(here[:, 8 * half : 8 * half + 8] * rows, axis=0)
-        gain_acc[:, at] = sums[0]
-        gain_acc[:, also] = sums[1]
+            sums = sums + jnp.sum((f32(part[z, :, :, :, at]) * f32(tokens[z, :, :, :, at])).reshape(16, 16, 256), axis=0)
+        gain_acc[:, at] = sums[:8]
+        gain_acc[:, also] = sums[8:]
         return carry
 
     lax.fori_loop(0, HALF // 256, gain_tile, 0)
@@ -411,17 +406,19 @@
             gain_copy(phase, by, moved(2 - phase, -by)).wait_recv()
         return (gain_slots[phase, 0] + gain_slots[phase, 1]) + (gain_slots[phase, 2] + gain_slots[phase, 3])
 
-    TILE = 512
+    TILE = 256
 
     def weight_tile(step, carry):
-        at = pl.ds(pl.multiple_of(step * TILE, TILE), TILE)
-        above, below = apart(tokens[:, :, :, :, at], TILE)
-        up_grad[at, :] = lax.dot_general(
-            above, weights[0].reshape(512, HID), (((0,), (0,)), ((), ())), preferred_element_type=jnp.float32
-        )
-        down_grad[:, at] = lax.dot_general(
-            weights[1].reshape(512, HID), below, (((0,), (0,)), ((), ())), preferred_element_type=jnp.float32
-        )
+        normed_at = pl.ds(pl.multiple_of(step * TILE, TILE), TILE)
+        grad_at = pl.ds(pl.multiple_of(HALF + step * TILE, TILE), TILE)
+        for half, rows in enumerate(apart(tokens[:, :, :, :, normed_at], TILE)):
+            up_grad[pl.ds(pl.multiple_of(half * HALF + step * TILE, TILE), TILE), :] = lax.dot_general(
+                rows, weights[0].reshape(512, HID), (((0,), (0,)), ((), ())), preferred_element_type=jnp.float32
+            )
+        for half, rows in enumerate(apart(tokens[:, :, :, :, grad_at], TILE)):
+            down_grad[:, pl.ds(pl.multiple_of(half * HALF + step * TILE, TILE), TILE)] = lax.dot_general(
+                weights[1].reshape(512, HID), rows, (((0,), (0,)), ((), ())), preferred_element_type=jnp.float32
+            )
         return carry
 
     gain_start(0)
@@ -447,7 +444,9 @@
         rs_sum(1, sub, 0)
     lax.fori_loop(13, 16, weight_tile, 0)
     gain_grad[...] = gain_sum(2)
-    own[...] = f32(tokens[place[1], place[0], (place[2] % 2) * 2 + place[2] // 2])[8:]
+    kept = f32(tokens[place[1], place[0], (place[2] % 2) * 2 + place[2] // 2, :, HALF:])
+    own[:, :HALF] = kept[:8]
+    own[:, HALF:] = kept[8:]
     for sub in SUBS:
         _, _, lo, size = SCATTER[sub]
         for by in (1, 2, 3):
@@ -515,8 +514,7 @@
             pltpu.VMEM((3, 4, 16, HALF), bf16),
             pltpu.VMEM((3, 16, HALF), bf16),
             pltpu.VMEM((4, 4, 4, 16, 2 * HID), f4),
-            pltpu.VMEM((ROWS, D), f4),
-            pltpu.VMEM((ROWS, D), f4),
+            pltpu.VMEM((16, HALF), bf16),
             pltpu.VMEM((ROWS, D), f4),
             pltpu.VMEM((3, 4, 1, D), f4),
             dma((3,)), dma((2,)),

time: 128 us -> 126 us (0.984)
  Pallas kernels: 127 us -> 125 us
    pallas_call x1, Pallas kernels: 121 us -> 119 us  [on_device(): pl.pallas_call(kernel, out_shape=[pltpu.VMEM((D, HID), f4), pltpu.VMEM((H...]
where the time goes in v5:
time: 126 us
  Pallas kernels  125 us (99%)
    pallas_call x1, Pallas kernels, on_device(): pl.pallas_call(kernel, out_shape=[pltpu.VMEM((D, HID), f4), pltpu.VMEM((H...  119 us
    pallas_call x1, Pallas kernels, on_device(): pl.pallas_call(finish, out_shape=[jax.ShapeDtypeStruct((ROWS, D), bf16),...  5.96 us

profile of v5, /device:TPU:0, one launch (start us, length us, event | category | flops | bytes accessed | tf_op | source)
XLA Modules:
  0.0 125.9 jit_solution(5571885254370288514)
XLA Ops:
  0.6 0.0 copy-start
  0.6 119.2 %section_backward.1 = (f32[8192,256]{1,0:T(8,128)S(1)}, f32[256,8192]{1,0:T(8,128)S(1)}, f32[8,8192]{1,0:T(8,128)S(1)}, f32[8,8192]{1,0:T(8,128)S(1)}, f32[8,128...) custom-call(bf16[8,8192]{1,0:T(8,128)(2,1)} %bitcast.9, bf16[8,8192]{1,0:T(8,128)(2,1)} %bitcast.10, ...), custom_call_target="tpu_custom_call" | custom-call | tf_op jit(solution)/shard_map/section_backward/pallas_call | solution.py:495
  119.8 0.0 copy-done
  119.8 6.0 %finish.1 = (bf16[8,8192]{1,0:T(8,128)(2,1)}, f32[1,8192]{1,0:T(1,128)}, f32[8192,256]{1,0:T(8,128)}, f32[256,8192]{1,0:T(8,128)}) custom-call(f32[8192,256]{1,0:T(8,128)S(1)} %get-tuple-element.15.up_grad, f32[256,8192]{1,0:T(8,128)S(1)} %get-tuple-element.16.down_grad, f32[8,8192]{1,0:T(8,128)S(1)} %get-tuple-element.17.total, ...), custom_call_target="tpu_custom_call" | custom-call | tf_op jit(solution)/shard_map/finish/pallas_call | solution.py:530
Async XLA Ops:
  0.6 119.2 %copy-start = (bf16[1,8192]{1,0:T(2,128)(2,1)S(1)}, bf16[1,8192]{1,0:T(2,128)(2,1)}, u32[]{:S(2)}) copy-start(bf16[1,8192]{1,0:T(2,128)(2,1)} %gain.3) | copy-start | bytes 49156

commit v6 on v5

--- a/solution.py
+++ b/solution.py
@@ -67,6 +67,11 @@
     def go(copy):
         copy.start()
         started.append(copy)
+
+    def settle(count):
+        for copy in started[:count]:
+            copy.wait_send()
+        del started[:count]
 
     def device_at(z, y, x):
         return (section, z * 2 + x % 2, y * 2 + x // 2)
@@ -242,15 +247,16 @@
 
     SWAPPED = (0, 2, 1, 3)
 
-    def activate(step, carry):
-        z, y = step // 4, step % 4
-        act, derivative = gelu_pair(hid[z, y, :, 0:8, 0:HID])
-        for x in range(4):
-            hid[z, y, x, 0:8, HID:] = hid[y, z, SWAPPED[x], 8:16, HID:] * derivative[x]
-            hid[z, y, x, 0:8, 0:HID] = act[x]
+    def activate(z, carry):
+        for y in range(4):
+            act, derivative = gelu_pair(hid[z, y, :, 0:8, 0:HID])
+            for x in range(4):
+                hid[z, y, x, 0:8, HID:] = hid[y, z, SWAPPED[x], 8:16, HID:] * derivative[x]
+                hid[z, y, x, 0:8, 0:HID] = act[x]
         return carry
 
-    lax.fori_loop(0, 16, activate, 0)
+    lax.fori_loop(0, 4, activate, 0)
+    gathers = len(started)
 
     def lay_out(step, carry):
         z, y = step // 4, step % 4
@@ -370,7 +376,9 @@
 
     line_step(0)
     lax.fori_loop(0, 16, lay_out, 0)
+    settle(gathers)
     line_step(1)
+    early = len(started)
     for sub in SUBS:
         second_products(sub, 0)
     line_sum(0)
@@ -424,14 +432,18 @@
     gain_start(0)
     line_sum(1)
     line_step(3)
-    lax.fori_loop(0, 6, weight_tile, 0)
+    late = len(started) - early
+    lax.fori_loop(0, 8, weight_tile, 0)
+    settle(early)
     gain_slots[1, place[1]] = gain_sum(0)
     gain_start(1)
     line_sum(2)
     for turn in range(4):
         for sub in SUBS:
             rs_forward(1, sub, far_first(sub)[turn])
-    lax.fori_loop(6, 13, weight_tile, 0)
+    second = len(started) - late
+    lax.fori_loop(8, 16, weight_tile, 0)
+    settle(late)
     gain_slots[2, place[0]] = gain_sum(1)
     gain_start(2)
     line_sum(3)
@@ -442,7 +454,7 @@
             go(last_copy(sub, unit_by % 4))
     for sub in SUBS:
         rs_sum(1, sub, 0)
-    lax.fori_loop(13, 16, weight_tile, 0)
+    settle(second)
     gain_grad[...] = gain_sum(2)
     kept = f32(tokens[place[1], place[0], (place[2] % 2) * 2 + place[2] // 2, :, HALF:])
     own[:, :HALF] = kept[:8]
@@ -457,8 +469,7 @@
             summed = summed + f32(got2[(by - 1, *columns)])
         total[:, pl.ds(lo, size)] = summed[:8]
         total[:, pl.ds(HALF + lo, size)] = summed[8:]
-    for copy in started:
-        copy.wait_send()
+    settle(len(started))
 
 
 def finish(

time: 126 us -> 125 us (level)
  no operation moved by 1% of the time
where the time goes in v6:
time: 125 us
  Pallas kernels  124 us (99%)
    pallas_call x1, Pallas kernels, on_device(): pl.pallas_call(kernel, out_shape=[pltpu.VMEM((D, HID), f4), pltpu.VMEM((H...  118 us
    pallas_call x1, Pallas kernels, on_device(): pl.pallas_call(finish, out_shape=[jax.ShapeDtypeStruct((ROWS, D), bf16),...  5.96 us

profile of v6, /device:TPU:0, one launch (start us, length us, event | category | flops | bytes accessed | tf_op | source)
XLA Modules:
  0.0 125.2 jit_solution(5016444540647379222)
XLA Ops:
  0.6 0.0 copy-start
  0.6 118.4 %section_backward.1 = (f32[8192,256]{1,0:T(8,128)S(1)}, f32[256,8192]{1,0:T(8,128)S(1)}, f32[8,8192]{1,0:T(8,128)S(1)}, f32[8,8192]{1,0:T(8,128)S(1)}, f32[8,128...) custom-call(bf16[8,8192]{1,0:T(8,128)(2,1)} %bitcast.9, bf16[8,8192]{1,0:T(8,128)(2,1)} %bitcast.10, ...), custom_call_target="tpu_custom_call" | custom-call | tf_op jit(solution)/shard_map/section_backward/pallas_call | solution.py:506
  119.0 0.0 copy-done
  119.0 6.0 %finish.1 = (bf16[8,8192]{1,0:T(8,128)(2,1)}, f32[1,8192]{1,0:T(1,128)}, f32[8192,256]{1,0:T(8,128)}, f32[256,8192]{1,0:T(8,128)}) custom-call(f32[8192,256]{1,0:T(8,128)S(1)} %get-tuple-element.15.up_grad, f32[256,8192]{1,0:T(8,128)S(1)} %get-tuple-element.16.down_grad, f32[8,8192]{1,0:T(8,128)S(1)} %get-tuple-element.17.total, ...), custom_call_target="tpu_custom_call" | custom-call | tf_op jit(solution)/shard_map/finish/pallas_call | solution.py:541
Async XLA Ops:
  0.6 118.4 %copy-start = (bf16[1,8192]{1,0:T(2,128)(2,1)S(1)}, bf16[1,8192]{1,0:T(2,128)(2,1)}, u32[]{:S(2)}) copy-start(bf16[1,8192]{1,0:T(2,128)(2,1)} %gain.3) | copy-start | bytes 49156

commit v7 on v6

--- a/solution.py
+++ b/solution.py
@@ -374,46 +374,6 @@
                 for unit_by in far_first(sub):
                     rs_start(1, sub, unit_by, turn)
 
-    line_step(0)
-    lax.fori_loop(0, 16, lay_out, 0)
-    settle(gathers)
-    line_step(1)
-    early = len(started)
-    for sub in SUBS:
-        second_products(sub, 0)
-    line_sum(0)
-    line_step(2)
-
-    def gain_tile(step, carry):
-        at = pl.ds(pl.multiple_of(step * 256, 256), 256)
-        also = pl.ds(pl.multiple_of(HALF + step * 256, 256), 256)
-        sums = jnp.zeros((16, 256), jnp.float32)
-        for z in range(4):
-            sums = sums + jnp.sum((f32(part[z, :, :, :, at]) * f32(tokens[z, :, :, :, at])).reshape(16, 16, 256), axis=0)
-        gain_acc[:, at] = sums[:8]
-        gain_acc[:, also] = sums[8:]
-        return carry
-
-    lax.fori_loop(0, HALF // 256, gain_tile, 0)
-    gain_slots[0, place[2]] = jnp.sum(gain_acc[...], axis=0, keepdims=True) / f32(gain[...])
-
-    def gain_copy(phase, by, owner):
-        axis = 2 - phase
-        return pltpu.make_async_remote_copy(
-            src_ref=gain_slots.at[phase, owner], dst_ref=gain_slots.at[phase, owner],
-            send_sem=gain_send.at[phase, by - 1], recv_sem=gain_recv.at[phase, by - 1],
-            device_id=neighbour(axis, by), device_id_type=MESH,
-        )
-
-    def gain_start(phase):
-        for by in (1, 2, 3):
-            go(gain_copy(phase, by, place[2 - phase]))
-
-    def gain_sum(phase):
-        for by in (1, 2, 3):
-            gain_copy(phase, by, moved(2 - phase, -by)).wait_recv()
-        return (gain_slots[phase, 0] + gain_slots[phase, 1]) + (gain_slots[phase, 2] + gain_slots[phase, 3])
-
     TILE = 256
 
     def weight_tile(step, carry):
@@ -429,11 +389,51 @@
             )
         return carry
 
+    lax.fori_loop(0, 16, lay_out, 0)
+    lax.fori_loop(0, 4, weight_tile, 0)
+    line_step(0)
+    settle(gathers)
+    line_step(1)
+    early = len(started)
+    for sub in SUBS:
+        second_products(sub, 0)
+    line_sum(0)
+    line_step(2)
+
+    def gain_tile(step, carry):
+        at = pl.ds(pl.multiple_of(step * 256, 256), 256)
+        also = pl.ds(pl.multiple_of(HALF + step * 256, 256), 256)
+        sums = jnp.zeros((16, 256), jnp.float32)
+        for z in range(4):
+            sums = sums + jnp.sum((f32(part[z, :, :, :, at]) * f32(tokens[z, :, :, :, at])).reshape(16, 16, 256), axis=0)
+        gain_acc[:, at] = sums[:8]
+        gain_acc[:, also] = sums[8:]
+        return carry
+
+    lax.fori_loop(0, HALF // 256, gain_tile, 0)
+    gain_slots[0, place[2]] = jnp.sum(gain_acc[...], axis=0, keepdims=True) / f32(gain[...])
+
+    def gain_copy(phase, by, owner):
+        axis = 2 - phase
+        return pltpu.make_async_remote_copy(
+            src_ref=gain_slots.at[phase, owner], dst_ref=gain_slots.at[phase, owner],
+            send_sem=gain_send.at[phase, by - 1], recv_sem=gain_recv.at[phase, by - 1],
+            device_id=neighbour(axis, by), device_id_type=MESH,
+        )
+
+    def gain_start(phase):
+        for by in (1, 2, 3):
+            go(gain_copy(phase, by, place[2 - phase]))
+
+    def gain_sum(phase):
+        for by in (1, 2, 3):
+            gain_copy(phase, by, moved(2 - phase, -by)).wait_recv()
+        return (gain_slots[phase, 0] + gain_slots[phase, 1]) + (gain_slots[phase, 2] + gain_slots[phase, 3])
+
     gain_start(0)
     line_sum(1)
     line_step(3)
-    late = len(started) - early
-    lax.fori_loop(0, 8, weight_tile, 0)
+    lax.fori_loop(4, 10, weight_tile, 0)
     settle(early)
     gain_slots[1, place[1]] = gain_sum(0)
     gain_start(1)
@@ -441,9 +441,8 @@
     for turn in range(4):
         for sub in SUBS:
             rs_forward(1, sub, far_first(sub)[turn])
-    second = len(started) - late
-    lax.fori_loop(8, 16, weight_tile, 0)
-    settle(late)
+    sent = len(started)
+    lax.fori_loop(10, 14, weight_tile, 0)
     gain_slots[2, place[0]] = gain_sum(1)
     gain_start(2)
     line_sum(3)
@@ -454,7 +453,8 @@
             go(last_copy(sub, unit_by % 4))
     for sub in SUBS:
         rs_sum(1, sub, 0)
-    settle(second)
+    lax.fori_loop(14, 16, weight_tile, 0)
+    settle(sent)
     gain_grad[...] = gain_sum(2)
     kept = f32(tokens[place[1], place[0], (place[2] % 2) * 2 + place[2] // 2, :, HALF:])
     own[:, :HALF] = kept[:8]

time: 125 us -> 125 us (level)
  no operation moved by 1% of the time
where the time goes in v7:
time: 125 us
  Pallas kernels  124 us (99%)
    pallas_call x1, Pallas kernels, on_device(): pl.pallas_call(kernel, out_shape=[pltpu.VMEM((D, HID), f4), pltpu.VMEM((H...  118 us
    pallas_call x1, Pallas kernels, on_device(): pl.pallas_call(finish, out_shape=[jax.ShapeDtypeStruct((ROWS, D), bf16),...  5.96 us

profile of v7, /device:TPU:0, one launch (start us, length us, event | category | flops | bytes accessed | tf_op | source)
XLA Modules:
  0.0 124.9 jit_solution(6920068598986630910)
XLA Ops:
  0.6 0.0 copy-start
  0.6 118.1 %section_backward.1 = (f32[8192,256]{1,0:T(8,128)S(1)}, f32[256,8192]{1,0:T(8,128)S(1)}, f32[8,8192]{1,0:T(8,128)S(1)}, f32[8,8192]{1,0:T(8,128)S(1)}, f32[8,128...) custom-call(bf16[8,8192]{1,0:T(8,128)(2,1)} %bitcast.9, bf16[8,8192]{1,0:T(8,128)(2,1)} %bitcast.10, ...), custom_call_target="tpu_custom_call" | custom-call | tf_op jit(solution)/shard_map/section_backward/pallas_call | solution.py:506
  118.8 0.0 copy-done
  118.8 6.0 %finish.1 = (bf16[8,8192]{1,0:T(8,128)(2,1)}, f32[1,8192]{1,0:T(1,128)}, f32[8192,256]{1,0:T(8,128)}, f32[256,8192]{1,0:T(8,128)}) custom-call(f32[8192,256]{1,0:T(8,128)S(1)} %get-tuple-element.15.up_grad, f32[256,8192]{1,0:T(8,128)S(1)} %get-tuple-element.16.down_grad, f32[8,8192]{1,0:T(8,128)S(1)} %get-tuple-element.17.total, ...), custom_call_target="tpu_custom_call" | custom-call | tf_op jit(solution)/shard_map/finish/pallas_call | solution.py:541
Async XLA Ops:
  0.6 118.1 %copy-start = (bf16[1,8192]{1,0:T(2,128)(2,1)S(1)}, bf16[1,8192]{1,0:T(2,128)(2,1)}, u32[]{:S(2)}) copy-start(bf16[1,8192]{1,0:T(2,128)(2,1)} %gain.3) | copy-start | bytes 49156

commit v8 on v7

--- a/solution.py
+++ b/solution.py
@@ -361,11 +361,12 @@
 
     def line_step(turn):
         for sub in SUBS:
-            rs_forward(0, sub, far_first(sub)[turn])
             if turn < 2:
                 rs_start(0, sub, far_first(sub)[turn + 2], 0)
             if 0 < turn < 3:
                 rs_start(0, sub, far_first(sub)[turn + 1], 1)
+        for sub in SUBS:
+            rs_forward(0, sub, far_first(sub)[turn])
 
     def line_sum(turn):
         for sub in SUBS:

time: 125 us -> 125 us (level)
  no operation moved by 1% of the time
where the time goes in v8:
time: 125 us
  Pallas kernels  124 us (99%)
    pallas_call x1, Pallas kernels, on_device(): pl.pallas_call(kernel, out_shape=[pltpu.VMEM((D, HID), f4), pltpu.VMEM((H...  118 us
    pallas_call x1, Pallas kernels, on_device(): pl.pallas_call(finish, out_shape=[jax.ShapeDtypeStruct((ROWS, D), bf16),...  5.96 us

profile of v8, /device:TPU:0, one launch (start us, length us, event | category | flops | bytes accessed | tf_op | source)
XLA Modules:
  0.0 125.0 jit_solution(7282670862903684385)
XLA Ops:
  0.6 0.0 copy-start
  0.6 118.2 %section_backward.1 = (f32[8192,256]{1,0:T(8,128)S(1)}, f32[256,8192]{1,0:T(8,128)S(1)}, f32[8,8192]{1,0:T(8,128)S(1)}, f32[8,8192]{1,0:T(8,128)S(1)}, f32[8,128...) custom-call(bf16[8,8192]{1,0:T(8,128)(2,1)} %bitcast.9, bf16[8,8192]{1,0:T(8,128)(2,1)} %bitcast.10, ...), custom_call_target="tpu_custom_call" | custom-call | tf_op jit(solution)/shard_map/section_backward/pallas_call | solution.py:507
  118.8 0.0 copy-done
  118.9 6.0 %finish.1 = (bf16[8,8192]{1,0:T(8,128)(2,1)}, f32[1,8192]{1,0:T(1,128)}, f32[8192,256]{1,0:T(8,128)}, f32[256,8192]{1,0:T(8,128)}) custom-call(f32[8192,256]{1,0:T(8,128)S(1)} %get-tuple-element.15.up_grad, f32[256,8192]{1,0:T(8,128)S(1)} %get-tuple-element.16.down_grad, f32[8,8192]{1,0:T(8,128)S(1)} %get-tuple-element.17.total, ...), custom_call_target="tpu_custom_call" | custom-call | tf_op jit(solution)/shard_map/finish/pallas_call | solution.py:542
Async XLA Ops:
  0.6 118.2 %copy-start = (bf16[1,8192]{1,0:T(2,128)(2,1)S(1)}, bf16[1,8192]{1,0:T(2,128)(2,1)}, u32[]{:S(2)}) copy-start(bf16[1,8192]{1,0:T(2,128)(2,1)} %gain.3) | copy-start | bytes 49156
